TPU v7x, 32 devices: a whole 2x2x4 slice. The times are simulated.
32 devices in a mesh: grp: 2 (over y), sta: 4 (over z), band: 4 (over x, core), src: 1.
Axes of the slice: x: 2, y: 2, z: 4, core: 2. Of those that a mesh axis runs over, the one named last changes fastest.
Arguments:
- spectra: float32 [1, 192, 1024], P('src', ('grp', 'sta', 'band')), parts along dimension 1, may hold values from -6 to 6
- station_place: int32 [192], P('grp'), parts along dimension 0, may hold values from 0 to 95, each once
- tiles: int32 [32, 2], P(('grp', 'sta', 'band')), parts along dimension 0, may hold values from 0 to 1
- observed: float32 [32, 48, 48, 256], P(('grp', 'sta', 'band')), parts along dimension 0, may hold values from -8 to 8
Outputs:
- adjoint: float32 [1, 192, 1024], P('src', ('grp', 'sta', 'band')), parts along dimension 1
There are 2 independent parts, one for each index of `grp`. A program takes and returns all parts, laid end to end along the dimension named above; each array names one. Nothing has to cross between parts.
Inputs may be any that keep to these rules, and one draw needn't show every extreme that they name: station_place is a permutation; block of station s is station_place[s] // 48.
All inputs are finite; a program needn't handle non-finite values.
Results may differ from a plain program's by a relative error of at most 0.00013.
Values sent between devices are 32-bit elements; how exact they have to be, the bound alone decides.
No kernel may reach another device: no remote copies, remote signals or barrier semaphores. Data moves between devices by JAX's collectives and lax.ppermute only.
A program may use at most 64 MiB of HBM per device.

v0:
```python
import math

import jax
import jax.numpy as jnp
from jax import lax
from jax.sharding import PartitionSpec as P

cubic_weight = 0.1


def dft_table(freqs, lags):
    fvals = jnp.arange(freqs, dtype=jnp.float32)
    tvals = jnp.arange(lags, dtype=jnp.float32) - lags // 2
    phase = math.pi / freqs * fvals[:, None] * tvals[None, :]
    return jnp.concatenate([jnp.cos(phase), -jnp.sin(phase)], 0) * (1.0 / math.sqrt(freqs))


def cross_spectrum(left, right):
    half = left.shape[-1] // 2
    lre = left[:, :, None, :half]
    lim = left[:, :, None, half:]
    rre = right[:, None, :, :half]
    rim = right[:, None, :, half:]
    real = jnp.sum(lre * rre + lim * rim, axis=0)
    imag = jnp.sum(lim * rre - lre * rim, axis=0)
    return jnp.concatenate([real, imag], -1)


def adjoint_terms(spectral, left, right):
    half = left.shape[-1] // 2
    are = spectral[:, :, :half]
    aim = spectral[:, :, half:]
    highest = lax.Precision.HIGHEST
    lre, lim = (left[:, :, :half], left[:, :, half:])
    rre, rim = (right[:, :, :half], right[:, :, half:])
    row_re = jnp.einsum("pqf,sqf->spf", are, rre, precision=highest) - jnp.einsum(
        "pqf,sqf->spf", aim, rim, precision=highest
    )
    row_im = jnp.einsum("pqf,sqf->spf", are, rim, precision=highest) + jnp.einsum(
        "pqf,sqf->spf", aim, rre, precision=highest
    )
    col_re = jnp.einsum("pqf,spf->sqf", are, lre, precision=highest) + jnp.einsum(
        "pqf,spf->sqf", aim, lim, precision=highest
    )
    col_im = jnp.einsum("pqf,spf->sqf", are, lim, precision=highest) - jnp.einsum(
        "pqf,spf->sqf", aim, lre, precision=highest
    )
    rows = jnp.concatenate([row_re, row_im], -1)
    cols = jnp.concatenate([col_re, col_im], -1)
    return jnp.concatenate([rows, cols], 1)


def local(spectra, station_place, tiles, observed):
    tile = observed.shape[1]
    lags = observed.shape[3]
    width = spectra.shape[2]
    slots = tiles.shape[0]
    count = station_place.shape[0]
    table = dft_table(width // 2, lags)
    highest = lax.Precision.HIGHEST
    whole = lax.all_gather(spectra[0], ("sta", "band"), axis=0, tiled=True)
    holder = (
        jnp.zeros((count,), jnp.int32).at[station_place].set(jnp.arange(count, dtype=jnp.int32))
    )
    offsets = jnp.arange(tile, dtype=jnp.int32)
    wanted = (tiles[:, :, None] * tile + offsets[None, None, :]).reshape(-1)
    fetched = jnp.take(whole, holder[wanted], axis=0).reshape(slots, 2, tile, width)
    slot = 0
    cross = cross_spectrum(fetched[slot, 0][None], fetched[slot, 1][None]).reshape(
        tile * tile, width
    )
    partial_lags = [jnp.dot(cross, table, precision=highest, preferred_element_type=jnp.float32)]
    lagged = lax.psum(jnp.stack(partial_lags, 0), "src")
    slot = 0
    misfit = lagged[slot] - observed[slot].reshape(tile * tile, lags)
    weighted = misfit + cubic_weight * misfit * misfit * misfit
    spectral = jnp.dot(weighted, table.T, precision=highest, preferred_element_type=jnp.float32)
    terms = adjoint_terms(
        spectral.reshape(tile, tile, width), fetched[slot, 0][None], fetched[slot, 1][None]
    )
    pieces = terms[0]
    select = (station_place[:, None] == wanted[None, :]).astype(jnp.float32)
    mine = lax.psum_scatter(
        jnp.dot(select, pieces, precision=highest, preferred_element_type=jnp.float32),
        ("sta", "band"),
        scatter_dimension=0,
        tiled=True,
    )
    return (mine * (1.0 / tile))[None]


def solution(mesh):
    placed = (
        P("src", ("grp", "sta", "band"), None),
        P("grp"),
        P(("grp", "sta", "band"), None),
        P(("grp", "sta", "band"), None, None, None),
    )
    return jax.shard_map(
        local,
        mesh=mesh,
        in_specs=placed,
        out_specs=P("src", ("grp", "sta", "band"), None),
        check_vma=False,
    )
```

profile of v0, /device:TPU:0, one launch (start us, length us, event | category | flops | bytes accessed | tf_op | source)
XLA Modules:
  0.0 95.4 jit_solution(15691845118605126946)
XLA Ops:
  0.0 0.7 multiply_bitcast_fusion
  0.7 0.1 add.110
  0.7 0.1 add.116
  0.8 0.1 add.118
  0.9 0.7 compare_select_fusion.3
  1.6 0.9 scatter_custom_fusion
  2.5 1.2 %gather_fusion = s32[96]{0:T(128)S(1)} fusion(s32[96]{0:T(128)S(1)} %scatter_custom_fusion, s32[1024]{0:T(1024)S(1)} %pad_clamp_fusion.1), kind=kCustom, calls=%fused_computation | custom fusion | bytes 1152 | tf_op jit(solution)/shard_map/gather | solution.py:67
  3.7 0.1 gather.14
  3.8 0.1 add.111
  3.9 24.4 %all-gather = f32[1,96,1024]{2,0,1:T(1,128)S(1)} all-gather(f32[1,6,1024]{2,0,1:T(1,128)} %param.4), channel_id=2, replica_groups=mesh['grp'=2,'sta'=4,'band'=4,'src'=1] {'sta','band'}, dimensions={1}, use_global_device_ids=true | all-gather | bytes 417792 | tf_op jit(solution)/shard_map/all_gather | solution.py:61
  28.3 0.1 copy.64
  28.3 0.7 gather_fusion.1
  29.1 0.1 broadcast_select_fusion
  29.2 0.1 add.113
  29.3 0.1 slice_bitcast_fusion.6
  29.4 1.9 %multiply_cosine_fusion = (f32[512,256]{1,0:T(8,128)S(1)}, f32[512,256]{1,0:T(8,128)S(1)}) fusion(f32[256]{0:T(256)S(1)} %iota_add_fusion, f32[512]{0:T(512)S(1)} %iota_multiply_fusion), kind=kLoop, calls=%fused_computation.24 | loop fusion | flops 262144 | bytes 1051648 | tf_op jit(solution)/shard_map/cos | solution.py:15
  31.3 1.5 %multiply_add_fusion = (f32[48,48,512]{2,1,0:T(8,128)S(1)}, f32[48,48,512]{2,1,0:T(8,128)S(1)}) fusion(f32[48,512]{1,0:T(8,128)S(1)} %get-tuple-element.32, f32[48,512]{1,0:T(8,128)S(1)} %get-tuple-element.27, f32[48,512]{1,0:T(8,128)S(1)} %get-tuple-element.31, f32[48,512]{1,0:T(8,128)S(1)} %get-tuple-element.28), kind=kLoop, calls=%fused_computation.16 | loop fusion | flops 7077888 | bytes 9830400 | tf_op jit(solution)/shard_map/add | solution.py:24
  32.8 8.3 %fusion.1 = f32[2304,256]{1,0:T(8,128)S(1)} fusion(f32[2304,512]{1,0:T(8,128)S(1)} %bitcast.101, f32[2304,512]{1,0:T(8,128)S(1)} %bitcast.100, f32[512,256]{1,0:T(8,128)S(1)} %get-tuple-element.30, f32[512,256]{1,0:T(8,128)S(1)} %get-tuple-element.29), kind=kOutput, calls=%fused_computation.3 | convolution fusion | flops 7250640896 | bytes 12845056 | tf_op jit(solution)/shard_map/dot_general | solution.py:72
  41.1 8.1 %fusion.5 = f32[48,48,1024]{2,1,0:T(8,128)S(1)} fusion(f32[48,48,256]{2,1,0:T(8,128)S(1)} %bitcast.102, f32[1,48,48,256]{3,2,1,0:T(8,128)S(1)} %copy-done, f32[512,256]{1,0:T(8,128)S(1)} %get-tuple-element.30, f32[512,256]{1,0:T(8,128)S(1)} %get-tuple-element.29), kind=kOutput, calls=%fused_computation.18 | convolution fusion | flops 7251230720 | bytes 15204352 | tf_op jit(solution)/shard_map/dot_general | solution.py:77
  49.2 3.1 %multiply_reduce_fusion.6 = (f32[512,48]{0,1:T(8,128)S(1)}, f32[512,48]{0,1:T(8,128)S(1)}, f32[512,48]{0,1:T(8,128)S(1)}, f32[512,48]{0,1:T(8,128)S(1)}) fusion(f32[48,48,1024]{2,1,0:T(8,128)S(1)} %fusion.5, f32[512,48]{0,1:T(8,128)S(1)} %get-tuple-element.33, f32[512,48]{0,1:T(8,128)S(1)} %get-tuple-element.34), kind=kLoop, calls=%fused_computation.13 | loop fusion | flops 9338880 | bytes 10027008 | tf_op jit(solution)/shard_map/pqf,sqf->spf/dot_general | solution.py:36
  52.4 0.0 copy-start.2
  52.4 1.7 %multiply_reduce_fusion.2 = (f32[512,48]{0,1:T(8,128)S(1)}, f32[512,48]{0,1:T(8,128)S(1)}, f32[512,48]{0,1:T(8,128)S(1)}, f32[512,48]{0,1:T(8,128)S(1)}) fusion(f32[48,48,1024]{2,1,0:T(8,128)S(1)} %fusion.5, f32[512,48]{0,1:T(8,128)S(1)} %get-tuple-element.26, f32[512,48]{0,1:T(8,128)S(1)} %get-tuple-element.25), kind=kLoop, calls=%fused_computation.9 | loop fusion | flops 9338880 | bytes 10027008 | tf_op jit(solution)/shard_map/pqf,spf->sqf/dot_general | solution.py:42
  54.2 0.4 fusion.11
  54.6 32.8 %fusion = f32[8,1024]{1,0:T(8,128)S(1)} fusion(f32[96,1024]{1,0:T(8,128)S(1)} %fusion.11), kind=kCustom, calls=%all-reduce-scatter | all-reduce-scatter fusion | flops 131073 | bytes 426496
  87.3 1.4 %collective-permute-start = (f32[8,1024]{1,0:T(8,128)S(1)}, f32[8,1024]{1,0:T(8,128)S(1)}, u32[]{:S(2)}, u32[]{:S(2)}) collective-permute-start(f32[8,1024]{1,0:T(8,128)S(1)} %fusion), channel_id=1, source_target_pairs={{0,1},{1,2},{2,3},{3,4},{4,5},{5,6},{6,7},{7,8},{8,9},{9,10},{10,1... | collective-permute-start | bytes 98312
  88.8 1.3 %collective-permute-start.1 = (f32[8,1024]{1,0:T(8,128)S(1)}, f32[8,1024]{1,0:T(8,128)S(1)}, u32[]{:S(2)}, u32[]{:S(2)}) collective-permute-start(f32[8,1024]{1,0:T(8,128)S(1)} %fusion), channel_id=1, source_target_pairs={{0,2},{1,3},{2,4},{3,5},{4,6},{5,7},{6,8},{7,9},{8,10},{9,11},{10,... | collective-permute-start | bytes 98312
  90.1 1.3 %collective-permute-start.2 = (f32[8,1024]{1,0:T(8,128)S(1)}, f32[8,1024]{1,0:T(8,128)S(1)}, u32[]{:S(2)}, u32[]{:S(2)}) collective-permute-start(f32[8,1024]{1,0:T(8,128)S(1)} %fusion), channel_id=1, source_target_pairs={{0,3},{1,4},{2,5},{3,6},{4,7},{5,8},{6,9},{7,10},{8,11},{9,12},{10... | collective-permute-start | bytes 98312
  91.4 1.3 %collective-permute-start.3 = (f32[6,1024]{1,0:T(8,128)S(1)}, f32[6,1024]{1,0:T(8,128)S(1)}, u32[]{:S(2)}, u32[]{:S(2)}) collective-permute-start(f32[6,1024]{1,0:T(8,128)S(1)} %slice.50), channel_id=1, source_target_pairs={{0,4},{1,5},{2,6},{3,7},{4,8},{5,9},{6,10},{7,11},{8,12},{9,13},{1... | collective-permute-start | bytes 73736
  92.7 0.6 dynamic-slice.4
  94.0 0.3 collective-permute-done.3
  94.3 0.4 concatenate.21
  94.8 0.6 copy.9
  (26 shorter events, 0.2 us)
Async XLA Ops:
  32.8 8.3 %copy-start = (f32[1,48,48,256]{3,2,1,0:T(8,128)S(1)}, f32[1,48,48,256]{3,2,1,0:T(8,128)}, u32[]{:S(2)}) copy-start(f32[1,48,48,256]{3,2,1,0:T(8,128)} %param.7) | copy-start | bytes 7077892
  52.4 1.8 %copy-start.1 = (s32[96]{0:T(128)S(1)}, s32[96]{0:T(128)}, u32[]{:S(2)}) copy-start(s32[96]{0:T(128)} %param.5) | copy-start | bytes 1156
  52.4 40.3 %copy-start.2 = (u32[32]{0:T(128)S(1)}, u32[32]{0:T(128)}, u32[]{:S(2)}) copy-start(u32[32]{0:T(128)} %constant.45) | copy-start | bytes 388
  87.3 6.9 %collective-permute-start = (f32[8,1024]{1,0:T(8,128)S(1)}, f32[8,1024]{1,0:T(8,128)S(1)}, u32[]{:S(2)}, u32[]{:S(2)}) collective-permute-start(f32[8,1024]{1,0:T(8,128)S(1)} %fusion), channel_id=1, source_target_pairs={{0,1},{1,2},{2,3},{3,4},{4,5},{5,6},{6,7},{7,8},{8,9},{9,10},{10,1... | collective-permute-start | bytes 98312
  88.8 5.5 %collective-permute-start.1 = (f32[8,1024]{1,0:T(8,128)S(1)}, f32[8,1024]{1,0:T(8,128)S(1)}, u32[]{:S(2)}, u32[]{:S(2)}) collective-permute-start(f32[8,1024]{1,0:T(8,128)S(1)} %fusion), channel_id=1, source_target_pairs={{0,2},{1,3},{2,4},{3,5},{4,6},{5,7},{6,8},{7,9},{8,10},{9,11},{10,... | collective-permute-start | bytes 98312
  90.1 4.2 %collective-permute-start.2 = (f32[8,1024]{1,0:T(8,128)S(1)}, f32[8,1024]{1,0:T(8,128)S(1)}, u32[]{:S(2)}, u32[]{:S(2)}) collective-permute-start(f32[8,1024]{1,0:T(8,128)S(1)} %fusion), channel_id=1, source_target_pairs={{0,3},{1,4},{2,5},{3,6},{4,7},{5,8},{6,9},{7,10},{8,11},{9,12},{10... | collective-permute-start | bytes 98312
  91.4 2.9 %collective-permute-start.3 = (f32[6,1024]{1,0:T(8,128)S(1)}, f32[6,1024]{1,0:T(8,128)S(1)}, u32[]{:S(2)}, u32[]{:S(2)}) collective-permute-start(f32[6,1024]{1,0:T(8,128)S(1)} %slice.50), channel_id=1, source_target_pairs={{0,4},{1,5},{2,6},{3,7},{4,8},{5,9},{6,10},{7,11},{8,12},{9,13},{1... | collective-permute-start | bytes 73736
where the time goes:
time: 97 us; the launch traced here: 95.4 us
  blocking collectives  57.1 us (59%)
  matrix products  16.7 us (17%)
  other arithmetic  9.75 us (10%)
  starting transfers between devices  5.32 us (5%)
  local copies, waits for them, and re-layouts  5.2 us (5%)
    unnamed x1, blocking collectives  32.8 us
    all_gather x1, blocking collectives, local(): whole = lax.all_gather(spectra[0], ('sta', 'band'), axis=0, tiled=True)  24.4 us
    dot_general x1, matrix products, local(): jnp.dot(cross, table, precision=highest, preferred_element_type=jnp.float32)  8.3 us
    dot_general x1, matrix products, local(): jnp.dot(weighted, table.T, precision=highest, preferred_element_type=jnp....  8.06 us
    unnamed x4, starting transfers between devices  5.32 us
    dot_general x1, other arithmetic, adjoint_terms(): jnp.einsum('pqf,sqf->spf', aim, rim, precision=highest)  3.14 us
  transfers between devices with their start and end apart: 4, of which 1 were waited for; matrix products, arithmetic and copies ran while one was open for 1% of the time, Pallas kernels for 0%

commit v1 on v0

v1 whole, which is shorter than its diff:
```python
import functools
import math

import jax
import jax.numpy as jnp
from jax import lax
from jax.experimental import pallas as pl
from jax.experimental.pallas import tpu as pltpu
from jax.sharding import PartitionSpec as P

cubic_weight = 0.1
LANES = 128
bf16 = jnp.bfloat16
f32 = jnp.float32


def dft_table(freqs, lags):
    fvals = jnp.arange(freqs, dtype=jnp.float32)
    tvals = jnp.arange(lags, dtype=jnp.float32) - lags // 2
    phase = math.pi / freqs * fvals[:, None] * tvals[None, :]
    return jnp.concatenate([jnp.cos(phase), -jnp.sin(phase)], 0) * (1.0 / math.sqrt(freqs))


def split(x):
    hi = x.astype(bf16)
    return hi, (x - hi.astype(f32)).astype(bf16)


def dot(a, b):
    return jnp.dot(a, b, preferred_element_type=f32)


def table_kernel(table, th, tl, bh, bl):
    value = table[...]
    th[...], tl[...] = split(value)
    bh[...], bl[...] = split(value.T)


def split_table(table):
    size, lags = table.shape
    shapes = [(size, lags), (size, lags), (lags, size), (lags, size)]
    return pl.pallas_call(
        table_kernel,
        out_shape=[jax.ShapeDtypeStruct(s, bf16) for s in shapes],
        cost_estimate=pl.CostEstimate(
            flops=8 * size * lags, bytes_accessed=12 * size * lags, transcendentals=0
        ),
    )(table)


def bits_of(n):
    return [1 << k for k in range(n.bit_length() - 1)]


def gather_order(sta, band):
    order = [(k, 0) for k in range(sta)]
    for bit in reversed(bits_of(band)):
        order = order + [(k, b ^ bit) for k, b in order]
    return order


def scatter_order(sta, band):
    bits = bits_of(band)
    inner = [0]
    for bit in bits[1:]:
        inner = inner + [b ^ bit for b in inner]
    order = [(k, b) for k in range(sta) for b in inner]
    for bit in bits[:1]:
        order = order + [(k, b ^ bit) for k, b in order]
    return order


def pairs(n, k):
    return [(i, i ^ k) for i in range(n)]


def gather(piece, sta, band):
    got = {k: lax.ppermute(piece, "sta", pairs(sta, k)) for k in range(sta - 1, 0, -1)}
    held = [piece] + [got[k] for k in range(1, sta)]
    for bit in reversed(bits_of(band)):
        whole = jnp.concatenate(held, 0) if len(held) > 1 else held[0]
        held = [whole, lax.ppermute(whole, "band", pairs(band, bit))]
    return held


def scatter_sum(parts, sta, band):
    bits = bits_of(band)
    total = parts[0]
    if bits:
        total = total + lax.ppermute(parts[1], "band", pairs(band, bits[0]))
    if sta > 1:
        each = total.shape[0] // sta
        sent = [
            lax.ppermute(total[k * each : (k + 1) * each], "sta", pairs(sta, k))
            for k in range(sta - 1, 0, -1)
        ]
        total = total[:each]
        for part in reversed(sent):
            total = total + part
    for bit in reversed(bits[1:]):
        half = total.shape[0] // 2
        total = total[:half] + lax.ppermute(total[half:], "band", pairs(band, bit))
    return total


def station_of(offset, me, band, rows):
    return ((offset[0] ^ me[0]) * band + (offset[1] ^ me[1])) * rows


def place_stations(held, place, me, blocked, geometry):
    sta, band, rows, per = geometry
    order = gather_order(sta, band)
    here = (me[0], me[1])
    at = 0
    for ref in held:
        for n in range(ref.shape[0] // (rows * per)):
            first = station_of(order[at], here, band, rows)
            at += 1
            for r in range(rows):
                to = pl.multiple_of(place[first + r] * per, per)
                blocked[pl.ds(to, per), :] = ref[(n * rows + r) * per : (n * rows + r + 1) * per, :]


def load_block(blocked, block, out, tile, per):
    view = blocked.at[pl.ds(pl.multiple_of(block * (tile * per), tile * per), tile * per)]
    for j in range(per):
        out[:, j * LANES : (j + 1) * LANES] = view[pl.ds(j, tile, stride=per), :]


def cross_rows(p0, count, ua, ub, xh, xl, tile, half):
    for c in range(half // LANES):
        re = slice(c * LANES, (c + 1) * LANES)
        im = slice(half + c * LANES, half + (c + 1) * LANES)
        bre, bim = ub[:, re], ub[:, im]
        ares, aims = ua[pl.ds(p0, count), re], ua[pl.ds(p0, count), im]
        for p in range(count):
            at = slice(p * tile, (p + 1) * tile)
            are, aim = ares[p : p + 1], aims[p : p + 1]
            xh[at, re], xl[at, re] = split(are * bre + aim * bim)
            xh[at, im], xl[at, im] = split(aim * bre - are * bim)


def lag_rows(xh, xl, th, tl):
    return dot(xh[...], th[...]) + (dot(xl[...], th[...]) + dot(xh[...], tl[...]))


def spectral_rows(lagged, seen, bh, bl):
    misfit = lagged - seen
    weighted = misfit + cubic_weight * misfit * misfit * misfit
    wh, wl = split(weighted)
    return dot(wh, bh[...]) + (dot(wl, bh[...]) + dot(wh, bl[...]))


def adjoint_rows(p0, count, spec, ua, ub, rows, cols, tile, half):
    for c in range(half // LANES):
        re = slice(c * LANES, (c + 1) * LANES)
        im = slice(half + c * LANES, half + (c + 1) * LANES)
        bre, bim = ub[:, re], ub[:, im]
        ares, aims = ua[pl.ds(p0, count), re], ua[pl.ds(p0, count), im]
        cre, cim = cols[:, re], cols[:, im]
        rre, rim = [], []
        for p in range(count):
            at = slice(p * tile, (p + 1) * tile)
            are, aim = ares[p : p + 1], aims[p : p + 1]
            sre, sim = spec[at, re], spec[at, im]
            rre.append(jnp.sum(sre * bre - sim * bim, axis=0, keepdims=True))
            rim.append(jnp.sum(sre * bim + sim * bre, axis=0, keepdims=True))
            cre = cre + (sre * are + sim * aim)
            cim = cim + (sre * aim - sim * are)
        cols[:, re] = cre
        cols[:, im] = cim
        rows[pl.ds(p0, count), re] = jnp.concatenate(rre, 0)
        rows[pl.ds(p0, count), im] = jnp.concatenate(rim, 0)


def give_terms(tiles, place, me, rows, cols, blocked, outs, geometry, tile):
    sta, band, nrows, per = geometry
    scale = 1.0 / tile
    blocked[...] = jnp.zeros_like(blocked)
    for block, ref in ((tiles[0, 0], rows), (tiles[0, 1], cols)):
        view = blocked.at[pl.ds(pl.multiple_of(block * (tile * per), tile * per), tile * per)]
        for j in range(per):
            spot = pl.ds(j, tile, stride=per)
            view[spot, :] = view[spot, :] + ref[:, j * LANES : (j + 1) * LANES]
    order = scatter_order(sta, band)
    here = (me[0], me[1])
    at = 0
    for out in outs:
        for n in range(out.shape[0] // (nrows * per)):
            first = station_of(order[at], here, band, nrows)
            at += 1
            for r in range(nrows):
                source = pl.multiple_of(place[first + r] * per, per)
                to = (n * nrows + r) * per
                out[to : to + per, :] = blocked[pl.ds(source, per), :] * scale


def tile_kernel(
    geometry, n_held, n_out, step, forward, backward, tiles, place, me, *refs
):
    held, refs = refs[:n_held], refs[n_held:]
    tile, half = None, None
    (th, tl, bh, bl), refs = refs[:4], refs[4:]
    per = geometry[3]
    half = th.shape[0] // 2
    lags = th.shape[1]
    if backward:
        observed, refs = refs[0], refs[1:]
        if not forward:
            given, refs = refs[0], refs[1:]
        outs, refs = refs[:n_out], refs[n_out:]
    else:
        lagged_out, refs = refs[0], refs[1:]
    blocked, ua, ub, xh, xl, spec, rows, cols = refs[:8]
    tile = ua.shape[0]
    if backward:
        seen, sem = refs[8:]
        fetch = pltpu.make_async_copy(observed.at[0], seen, sem)
        fetch.start()
    place_stations(held, place, me, blocked, geometry)
    load_block(blocked, tiles[0, 0], ua, tile, per)
    load_block(blocked, tiles[0, 1], ub, tile, per)
    if backward:
        cols[...] = jnp.zeros_like(cols)
        fetch.wait()

    def body(i, carry):
        p0 = pl.multiple_of(i * step, step)
        m0 = pl.multiple_of(i * (step * tile), step * tile)
        if forward:
            cross_rows(p0, step, ua, ub, xh, xl, tile, half)
            lagged = lag_rows(xh, xl, th, tl)
        else:
            lagged = given[pl.ds(m0, step * tile), :]
        if not backward:
            lagged_out[pl.ds(m0, step * tile), :] = lagged
            return carry
        look = seen[pl.ds(p0, step)].reshape(step * tile, lags)
        spec[...] = spectral_rows(lagged, look, bh, bl)
        adjoint_rows(p0, step, spec, ua, ub, rows, cols, tile, half)
        return carry

    lax.fori_loop(0, tile // step, body, 0)
    if backward:
        give_terms(tiles, place, me, rows, cols, blocked, outs, geometry, tile)


def tile_call(geometry, tiles, place, me, held, tables, observed, lagged=None, forward=True, backward=True):
    sta, band, rows, per = geometry
    tile, lags = observed.shape[2], observed.shape[3]
    width = per * LANES
    step = 8
    count = place.shape[0]
    smem = pl.BlockSpec(memory_space=pltpu.SMEM)
    vmem = pl.BlockSpec(memory_space=pltpu.VMEM)
    anys = pl.BlockSpec(memory_space=pl.ANY)
    args = [tiles, place, me, *held, *tables]
    specs = [smem] * 3 + [vmem] * (len(held) + 4)
    n_out = 2 if band > 1 else 1
    scratch = [
        pltpu.VMEM((count * per, LANES), f32),
        pltpu.VMEM((tile, width), f32),
        pltpu.VMEM((tile, width), f32),
        pltpu.VMEM((step * tile, width), bf16),
        pltpu.VMEM((step * tile, width), bf16),
        pltpu.VMEM((step * tile, width), f32),
        pltpu.VMEM((tile, width), f32),
        pltpu.VMEM((tile, width), f32),
    ]
    if backward:
        args.append(observed)
        specs.append(anys)
        if not forward:
            args.append(lagged)
            specs.append(vmem)
        out_shape = [jax.ShapeDtypeStruct((count * per // n_out, LANES), f32)] * n_out
        scratch += [pltpu.VMEM((tile, tile, lags), f32), pltpu.SemaphoreType.DMA]
    else:
        out_shape = [jax.ShapeDtypeStruct((tile * tile, lags), f32)]
    pairs_count = tile * tile
    return pl.pallas_call(
        functools.partial(tile_kernel, geometry, len(held), n_out, step, forward, backward),
        in_specs=specs,
        out_specs=[vmem] * len(out_shape),
        out_shape=out_shape,
        scratch_shapes=scratch,
        compiler_params=pltpu.CompilerParams(vmem_limit_bytes=32 * 2**20),
        cost_estimate=pl.CostEstimate(
            flops=12 * pairs_count * width * lags, bytes_accessed=16 * pairs_count * lags, transcendentals=0
        ),
    )(*args)


def local(sizes, spectra, place, tiles, observed):
    sta, band, src = sizes
    width = spectra.shape[2]
    rows = spectra.shape[1]
    per = width // LANES
    geometry = (sta, band, rows, per)
    piece = spectra.reshape(rows * per, LANES)
    held = gather(piece, sta, band)
    me = jnp.stack([lax.axis_index("sta"), lax.axis_index("band")]).astype(jnp.int32)
    tables = split_table(dft_table(width // 2, observed.shape[3]))
    if src == 1:
        parts = tile_call(geometry, tiles, place, me, held, tables, observed)
    else:
        (lagged,) = tile_call(geometry, tiles, place, me, held, tables, observed, backward=False)
        lagged = lax.psum(lagged, "src")
        parts = tile_call(geometry, tiles, place, me, held, tables, observed, lagged, forward=False)
    return scatter_sum(parts, sta, band).reshape(spectra.shape)


def solution(mesh):
    placed = (
        P("src", ("grp", "sta", "band"), None),
        P("grp"),
        P(("grp", "sta", "band"), None),
        P(("grp", "sta", "band"), None, None, None),
    )
    sizes = tuple(mesh.shape[name] for name in ("sta", "band", "src"))
    return jax.shard_map(
        functools.partial(local, sizes),
        mesh=mesh,
        in_specs=placed,
        out_specs=P("src", ("grp", "sta", "band"), None),
        check_vma=False,
    )
```

time: 97 us -> 59.6 us (0.61); the launches traced: 95.4 us -> 59.1 us
  blocking collectives: 57.1 us -> 0 us
  Pallas kernels: 0 us -> 21.3 us
  matrix products: 16.7 us -> 0 us
  waiting for transfers between devices: 0.34 us -> 12.4 us
  starting transfers between devices: 5.32 us -> 13.8 us
  other arithmetic: 9.75 us -> 6.57 us
    unnamed x1 -> x0, blocking collectives: 32.8 us -> none
    all_gather x1 -> x0, blocking collectives: 24.4 us -> none  [local(): whole = lax.all_gather(spectra[0], ('sta', 'band'), axis=0, tiled=True)]
    pallas_call x0 -> x2, Pallas kernels: none -> 21.3 us  [the longest x1 18.6 us: tile_call(): pl.pallas_call(functools.partial(tile_kernel, geometry, len(held), n_out,...]
    dot_general x3 -> x0, matrix products: 16.7 us -> none  [the longest x1 8.3 us: local(): jnp.dot(cross, table, precision=highest, preferred_element_type=jnp.float32)]
    ppermute x0 -> x10, starting transfers between devices: none -> 13.8 us  [the longest x3 5.62 us: gather(): lax.ppermute(piece, 'sta', pairs(sta, k))]
    ppermute x0 -> x10, waiting for transfers between devices: none -> 12.4 us  [the longest x3 3.82 us: scatter_sum(): lax.ppermute(total[k * each:(k + 1) * each], 'sta', pairs(sta, k))]
    unnamed x4 -> x0, starting transfers between devices: 5.32 us -> none
    dot_general x2 -> x0, other arithmetic: 4.82 us -> none  [the longest x1 3.14 us: adjoint_terms(): jnp.einsum('pqf,sqf->spf', aim, rim, precision=highest)]
  transfers between devices with their start and end apart: 4 -> 10, of which waited for: 1 -> 7; matrix products, arithmetic and copies ran while one was open for 1% -> 10% of each run, Pallas kernels for 0% -> 5%
where the time goes in v1:
time: 59.6 us; the launch traced here: 59.1 us
  Pallas kernels  21.3 us (36%)
  starting transfers between devices  13.8 us (23%)
  waiting for transfers between devices  12.4 us (21%)
  other arithmetic  6.57 us (11%)
  local copies, waits for them, and re-layouts  4.95 us (8%)
    pallas_call x1, Pallas kernels, tile_call(): pl.pallas_call(functools.partial(tile_kernel, geometry, len(held), n_out,...  18.6 us
    ppermute x3, starting transfers between devices, gather(): lax.ppermute(piece, 'sta', pairs(sta, k))  5.62 us
    unnamed x18, local copies, waits for them, and re-layouts  4.92 us
    ppermute x3, starting transfers between devices, scatter_sum(): lax.ppermute(total[k * each:(k + 1) * each], 'sta', pairs(sta, k))  4.46 us
    ppermute x3, waiting for transfers between devices, scatter_sum(): lax.ppermute(total[k * each:(k + 1) * each], 'sta', pairs(sta, k))  3.82 us
    ppermute x2, waiting for transfers between devices, gather(): held = [whole, lax.ppermute(whole, 'band', pairs(band, bit))]  3.11 us
    cos x1, other arithmetic, dft_table(): jnp.cos(phase)  2.96 us
    pallas_call x1, Pallas kernels, split_table(): pl.pallas_call(table_kernel, out_shape=[jax.ShapeDtypeStruct(s, bf16) for...  2.77 us
  transfers between devices with their start and end apart: 10, of which 7 were waited for; matrix products, arithmetic and copies ran while one was open for 10% of the time, Pallas kernels for 5%

profile of v1, /device:TPU:0, one launch (start us, length us, event | category | flops | bytes accessed | tf_op | source)
XLA Modules:
  0.0 59.1 jit_solution(11335522787520480603)
XLA Ops:
  0.0 3.0 %collective-permute-start = (f32[48,128]{1,0:T(8,128)}, f32[48,128]{1,0:T(8,128)S(1)}, u32[]{:S(2)}, u32[]{:S(2)}) collective-permute-start(f32[48,128]{1,0:T(8,128)} %bitcast.4), channel_id=1, source_target_pairs={{0,4},{4,0},{8,12},{12,8},{1,5},{5,1},{9,13},{13,9},{2,6},{6,2},{1... | collective-permute-start | bytes 73736 | tf_op jit(solution)/shard_map/ppermute | solution.py:78
  3.0 2.6 %collective-permute-start.1 = (f32[48,128]{1,0:T(8,128)}, f32[48,128]{1,0:T(8,128)S(1)}, u32[]{:S(2)}, u32[]{:S(2)}) collective-permute-start(f32[48,128]{1,0:T(8,128)} %bitcast.5), channel_id=1, source_target_pairs={{0,8},{4,12},{8,0},{12,4},{1,9},{5,13},{9,1},{13,5},{2,10},{6,14},... | collective-permute-start | bytes 73736 | tf_op jit(solution)/shard_map/ppermute | solution.py:78
  5.6 0.0 collective-permute-start.2
  5.6 0.0 copy-start.5
  5.7 0.0 copy-start.6
  5.7 3.0 %multiply_cosine_fusion = (f32[512,256]{1,0:T(8,128)S(1)}, f32[512,256]{1,0:T(8,128)}) fusion(f32[256]{0:T(256)S(1)} %iota_add_fusion, f32[512]{0:T(512)S(1)} %iota_multiply_fusion), kind=kLoop, calls=%fused_computation.2 | loop fusion | flops 262144 | bytes 1051648 | tf_op jit(solution)/shard_map/cos | solution.py:21
  8.6 0.7 %constant_dynamic-update-slice_fusion.4 = f32[384,128]{1,0:T(8,128)S(1)} fusion(f32[48,128]{1,0:T(8,128)} %bitcast.7), kind=kLoop, calls=%fused_computation.13 | loop fusion | bytes 49152
  9.4 0.0 collective-permute-done
  9.4 2.1 %collective-permute-done.2 = f32[48,128]{1,0:T(8,128)S(1)} collective-permute-done((f32[48,128]{1,0:T(8,128)}, f32[48,128]{1,0:T(8,128)S(1)}, u32[]{:S(2)}, u32[]{:S(2)}) %collective-permute-start.2) | collective-permute-done | bytes 24608 | tf_op jit(solution)/shard_map/ppermute | solution.py:78
  11.4 0.7 %pad_maximum_fusion = f32[192,128]{1,0:T(8,128)S(1)} fusion(f32[48,128]{1,0:T(8,128)S(1)} %collective-permute-done.2, f32[48,128]{1,0:T(8,128)S(1)} %collective-permute-done.1, f32[48,128]{1,0:T(8,128)S(1)} %collective-permute-done, f32[48,128]{1,0:T(8,128)} %bitcast.8), kind=kLoop, calls=%fused_computation.4 | loop fusion | flops 73728 | bytes 196608 | tf_op jit(solution)/shard_map/concatenate | solution.py:81
  12.2 1.5 %collective-permute-start.3 = (f32[192,128]{1,0:T(8,128)S(1)}, f32[192,128]{1,0:T(8,128)S(1)}, u32[]{:S(2)}, u32[]{:S(2)}) collective-permute-start(f32[192,128]{1,0:T(8,128)S(1)} %pad_maximum_fusion), channel_id=1, source_target_pairs={{0,2},{1,3},{2,0},{3,1},{4,6},{5,7},{6,4},{7,5},{8,10},{9,11},{10,... | collective-permute-start | bytes 294920 | tf_op jit(solution)/shard_map/ppermute | solution.py:82
  13.7 3.1 %collective-permute-done.3 = f32[192,128]{1,0:T(8,128)S(1)} collective-permute-done((f32[192,128]{1,0:T(8,128)S(1)}, f32[192,128]{1,0:T(8,128)S(1)}, u32[]{:S(2)}, u32[]{:S(2)}) %collective-permute-start.3) | collective-permute-done | bytes 98336 | tf_op jit(solution)/shard_map/ppermute | solution.py:82
  16.8 0.1 collective-permute-start.4
  16.9 2.1 %maximum_multiply_fusion.table = f32[1024,256]{1,0:T(8,128)} fusion(f32[512,256]{1,0:T(8,128)} %get-tuple-element.21, f32[512,256]{1,0:T(8,128)S(1)} %get-tuple-element.20), kind=kLoop, calls=%fused_computation | loop fusion | flops 524288 | bytes 2097152 | tf_op jit(solution)/shard_map/mul | solution.py:21
  19.0 2.8 %shard_map.46 = (bf16[1024,256]{1,0:T(8,128)(2,1)}, bf16[1024,256]{1,0:T(8,128)(2,1)}, bf16[256,1024]{1,0:T(8,128)(2,1)}, bf16[256,1024]{1,0:T(8,128)(2,1)}) custom-call(f32[1024,256]{1,0:T(8,128)} %maximum_multiply_fusion.table), custom_call_target="tpu_custom_call" | custom-call | flops 2097152 | bytes 3145728 | tf_op jit(solution)/shard_map/pallas_call | solution.py:42
  21.8 0.1 pad_add_fusion.me
  21.9 1.0 %copy-done.1 = bf16[1024,256]{1,0:T(8,128)(2,1)S(1)} copy-done((bf16[1024,256]{1,0:T(8,128)(2,1)S(1)}, bf16[1024,256]{1,0:T(8,128)(2,1)}, u32[]{:S(2)}) %copy-start.1) | copy-done | bytes 524312
  22.9 1.0 %copy-done.2 = bf16[1024,256]{1,0:T(8,128)(2,1)S(1)} copy-done((bf16[1024,256]{1,0:T(8,128)(2,1)S(1)}, bf16[1024,256]{1,0:T(8,128)(2,1)}, u32[]{:S(2)}) %copy-start.2) | copy-done | bytes 524312
  24.0 1.0 %copy-done.3 = bf16[256,1024]{1,0:T(8,128)(2,1)S(1)} copy-done((bf16[256,1024]{1,0:T(8,128)(2,1)S(1)}, bf16[256,1024]{1,0:T(8,128)(2,1)}, u32[]{:S(2)}) %copy-start.3) | copy-done | bytes 524312
  25.0 1.0 %copy-done.4 = bf16[256,1024]{1,0:T(8,128)(2,1)S(1)} copy-done((bf16[256,1024]{1,0:T(8,128)(2,1)S(1)}, bf16[256,1024]{1,0:T(8,128)(2,1)}, u32[]{:S(2)}) %copy-start.4) | copy-done | bytes 524312
  26.1 18.6 %shard_map.47 = (f32[384,128]{1,0:T(8,128)S(1)}, f32[384,128]{1,0:T(8,128)S(1)}) custom-call(s32[1,2]{1,0:T(1,128)S(1)} %copy-done.5, s32[96]{0:T(128)S(1)} %copy-done.6, s32[2]{0:T(128)S(1)} %pad_add_fusion.me, f32[384,128]{1,0:T(8,128)S(1)} %constant_dynamic-update-slice_fusion.refs_0_, f32[384,128]{1,0:T(8,128)S(1)} %collective-permute-done.4.refs_1_, ...), custom_call_target="tpu_custom_call" | custom-call | flops 7247757312 | bytes 9437184 | tf_op jit(solution)/shard_map/pallas_call | solution.py:281
  44.6 0.6 collective-permute-start.5
  45.2 1.1 %collective-permute-done.5 = f32[384,128]{1,0:T(8,128)S(1)} collective-permute-done((f32[384,128]{1,0:T(8,128)S(1)}, f32[384,128]{1,0:T(8,128)S(1)}, u32[]{:S(2)}, u32[]{:S(2)}) %collective-permute-start.5) | collective-permute-done | bytes 196640 | tf_op jit(solution)/shard_map/ppermute | solution.py:90
  46.3 0.1 collective-permute-start.6
  46.4 2.3 %collective-permute-start.7 = (f32[96,128]{1,0:T(8,128)S(1)}, f32[96,128]{1,0:T(8,128)S(1)}, u32[]{:S(2)}, u32[]{:S(2)}) collective-permute-start(f32[96,128]{1,0:T(8,128)S(1)} %get-tuple-element.19), channel_id=1, source_target_pairs={{0,8},{4,12},{8,0},{12,4},{1,9},{5,13},{9,1},{13,5},{2,10},{6,14},... | collective-permute-start | bytes 147464 | tf_op jit(solution)/shard_map/ppermute | solution.py:94
  48.7 2.1 %collective-permute-start.8 = (f32[96,128]{1,0:T(8,128)S(1)}, f32[96,128]{1,0:T(8,128)S(1)}, u32[]{:S(2)}, u32[]{:S(2)}) collective-permute-start(f32[96,128]{1,0:T(8,128)S(1)} %get-tuple-element.18), channel_id=1, source_target_pairs={{0,12},{4,8},{8,4},{12,0},{1,13},{5,9},{9,5},{13,1},{2,14},{6,10},... | collective-permute-start | bytes 147464 | tf_op jit(solution)/shard_map/ppermute | solution.py:94
  50.8 0.3 collective-permute-done.6
  51.1 2.4 %collective-permute-done.7 = f32[96,128]{1,0:T(8,128)S(1)} collective-permute-done((f32[96,128]{1,0:T(8,128)S(1)}, f32[96,128]{1,0:T(8,128)S(1)}, u32[]{:S(2)}, u32[]{:S(2)}) %collective-permute-start.7) | collective-permute-done | bytes 49184 | tf_op jit(solution)/shard_map/ppermute | solution.py:94
  53.5 1.1 %collective-permute-done.8 = f32[96,128]{1,0:T(8,128)S(1)} collective-permute-done((f32[96,128]{1,0:T(8,128)S(1)}, f32[96,128]{1,0:T(8,128)S(1)}, u32[]{:S(2)}, u32[]{:S(2)}) %collective-permute-start.8) | collective-permute-done | bytes 49184 | tf_op jit(solution)/shard_map/ppermute | solution.py:94
  54.6 1.6 %collective-permute-start.9 = (f32[48,128]{1,0:T(8,128)S(1)}, f32[48,128]{1,0:T(8,128)S(1)}, u32[]{:S(2)}, u32[]{:S(2)}) collective-permute-start(f32[48,128]{1,0:T(8,128)S(1)} %slice.29), channel_id=1, source_target_pairs={{0,2},{1,3},{2,0},{3,1},{4,6},{5,7},{6,4},{7,5},{8,10},{9,11},{10,... | collective-permute-start | bytes 73736 | tf_op jit(solution)/shard_map/ppermute | solution.py:102
  56.2 2.3 %collective-permute-done.9 = f32[48,128]{1,0:T(8,128)S(1)} collective-permute-done((f32[48,128]{1,0:T(8,128)S(1)}, f32[48,128]{1,0:T(8,128)S(1)}, u32[]{:S(2)}, u32[]{:S(2)}) %collective-permute-start.9) | collective-permute-done | bytes 24608 | tf_op jit(solution)/shard_map/ppermute | solution.py:102
  58.5 0.6 %slice_add_fusion.1 = f32[48,128]{1,0:T(8,128)} fusion(f32[48,128]{1,0:T(8,128)S(1)} %collective-permute-done.9, f32[96,128]{1,0:T(8,128)S(1)} %fusion.2), kind=kLoop, calls=%fused_computation.8 | loop fusion | flops 6144 | bytes 73728 | tf_op jit(solution)/shard_map/add | solution.py:102
  (20 shorter events, 0.1 us)
Async XLA Ops:
  0.0 9.4 %collective-permute-start = (f32[48,128]{1,0:T(8,128)}, f32[48,128]{1,0:T(8,128)S(1)}, u32[]{:S(2)}, u32[]{:S(2)}) collective-permute-start(f32[48,128]{1,0:T(8,128)} %bitcast.4), channel_id=1, source_target_pairs={{0,4},{4,0},{8,12},{12,8},{1,5},{5,1},{9,13},{13,9},{2,6},{6,2},{1... | collective-permute-start | bytes 73736 | tf_op jit(solution)/shard_map/ppermute | solution.py:78
  3.0 6.3 %collective-permute-start.1 = (f32[48,128]{1,0:T(8,128)}, f32[48,128]{1,0:T(8,128)S(1)}, u32[]{:S(2)}, u32[]{:S(2)}) collective-permute-start(f32[48,128]{1,0:T(8,128)} %bitcast.5), channel_id=1, source_target_pairs={{0,8},{4,12},{8,0},{12,4},{1,9},{5,13},{9,1},{13,5},{2,10},{6,14},... | collective-permute-start | bytes 73736 | tf_op jit(solution)/shard_map/ppermute | solution.py:78
  5.6 5.8 %collective-permute-start.2 = (f32[48,128]{1,0:T(8,128)}, f32[48,128]{1,0:T(8,128)S(1)}, u32[]{:S(2)}, u32[]{:S(2)}) collective-permute-start(f32[48,128]{1,0:T(8,128)} %bitcast.6), channel_id=1, source_target_pairs={{0,12},{4,8},{8,4},{12,0},{1,13},{5,9},{9,5},{13,1},{2,14},{6,10},... | collective-permute-start | bytes 73736 | tf_op jit(solution)/shard_map/ppermute | solution.py:78
  5.6 16.2 %copy-start = (f32[1,48,48,256]{3,2,1,0:T(8,128)S(1)}, f32[1,48,48,256]{3,2,1,0:T(8,128)}, u32[]{:S(2)}) copy-start(f32[1,48,48,256]{3,2,1,0:T(8,128)} %refs_6_.1) | copy-start | bytes 7077892
  5.6 16.2 %copy-start.5 = (s32[1,2]{1,0:T(1,128)S(1)}, s32[1,2]{1,0:T(1,128)}, u32[]{:S(2)}) copy-start(s32[1,2]{1,0:T(1,128)} %tiles.1) | copy-start | bytes 28
  5.7 16.2 %copy-start.6 = (s32[96]{0:T(128)S(1)}, s32[96]{0:T(128)}, u32[]{:S(2)}) copy-start(s32[96]{0:T(128)} %place.1) | copy-start | bytes 1156
  12.2 4.6 %collective-permute-start.3 = (f32[192,128]{1,0:T(8,128)S(1)}, f32[192,128]{1,0:T(8,128)S(1)}, u32[]{:S(2)}, u32[]{:S(2)}) collective-permute-start(f32[192,128]{1,0:T(8,128)S(1)} %pad_maximum_fusion), channel_id=1, source_target_pairs={{0,2},{1,3},{2,0},{3,1},{4,6},{5,7},{6,4},{7,5},{8,10},{9,11},{10,... | collective-permute-start | bytes 294920 | tf_op jit(solution)/shard_map/ppermute | solution.py:82
  16.8 5.1 %collective-permute-start.4 = (f32[384,128]{1,0:T(8,128)S(1)}, f32[384,128]{1,0:T(8,128)S(1)}, u32[]{:S(2)}, u32[]{:S(2)}) collective-permute-start(f32[384,128]{1,0:T(8,128)S(1)} %constant_dynamic-update-slice_fusion.refs_0_), channel_id=1, source_target_pairs={{0,1},{1,0},{2,3},{3,2},{4,5},{5,4},{6,7},{7,6},{8,9},{9,8},{10,11... | collective-permute-start | bytes 589832 | tf_op jit(solution)/shard_map/ppermute | solution.py:82
  21.9 1.0 %copy-start.1 = (bf16[1024,256]{1,0:T(8,128)(2,1)S(1)}, bf16[1024,256]{1,0:T(8,128)(2,1)}, u32[]{:S(2)}) copy-start(bf16[1024,256]{1,0:T(8,128)(2,1)} %get-tuple-element.11.refs_2_) | copy-start | bytes 1572868
  22.9 1.0 %copy-start.2 = (bf16[1024,256]{1,0:T(8,128)(2,1)S(1)}, bf16[1024,256]{1,0:T(8,128)(2,1)}, u32[]{:S(2)}) copy-start(bf16[1024,256]{1,0:T(8,128)(2,1)} %get-tuple-element.12.refs_3_) | copy-start | bytes 1572868
  24.0 1.0 %copy-start.3 = (bf16[256,1024]{1,0:T(8,128)(2,1)S(1)}, bf16[256,1024]{1,0:T(8,128)(2,1)}, u32[]{:S(2)}) copy-start(bf16[256,1024]{1,0:T(8,128)(2,1)} %get-tuple-element.13.refs_4_) | copy-start | bytes 1572868
  25.0 1.0 %copy-start.4 = (bf16[256,1024]{1,0:T(8,128)(2,1)S(1)}, bf16[256,1024]{1,0:T(8,128)(2,1)}, u32[]{:S(2)}) copy-start(bf16[256,1024]{1,0:T(8,128)(2,1)} %get-tuple-element.14.refs_5_) | copy-start | bytes 1572868
  44.6 1.6 %collective-permute-start.5 = (f32[384,128]{1,0:T(8,128)S(1)}, f32[384,128]{1,0:T(8,128)S(1)}, u32[]{:S(2)}, u32[]{:S(2)}) collective-permute-start(f32[384,128]{1,0:T(8,128)S(1)} %get-tuple-element.16), channel_id=1, source_target_pairs={{0,1},{1,0},{2,3},{3,2},{4,5},{5,4},{6,7},{7,6},{8,9},{9,8},{10,11... | collective-permute-start | bytes 589832 | tf_op jit(solution)/shard_map/ppermute | solution.py:90
  46.3 4.8 %collective-permute-start.6 = (f32[96,128]{1,0:T(8,128)S(1)}, f32[96,128]{1,0:T(8,128)S(1)}, u32[]{:S(2)}, u32[]{:S(2)}) collective-permute-start(f32[96,128]{1,0:T(8,128)S(1)} %get-tuple-element.17), channel_id=1, source_target_pairs={{0,4},{4,0},{8,12},{12,8},{1,5},{5,1},{9,13},{13,9},{2,6},{6,2},{1... | collective-permute-start | bytes 147464 | tf_op jit(solution)/shard_map/ppermute | solution.py:94
  46.4 7.1 %collective-permute-start.7 = (f32[96,128]{1,0:T(8,128)S(1)}, f32[96,128]{1,0:T(8,128)S(1)}, u32[]{:S(2)}, u32[]{:S(2)}) collective-permute-start(f32[96,128]{1,0:T(8,128)S(1)} %get-tuple-element.19), channel_id=1, source_target_pairs={{0,8},{4,12},{8,0},{12,4},{1,9},{5,13},{9,1},{13,5},{2,10},{6,14},... | collective-permute-start | bytes 147464 | tf_op jit(solution)/shard_map/ppermute | solution.py:94
  48.7 5.9 %collective-permute-start.8 = (f32[96,128]{1,0:T(8,128)S(1)}, f32[96,128]{1,0:T(8,128)S(1)}, u32[]{:S(2)}, u32[]{:S(2)}) collective-permute-start(f32[96,128]{1,0:T(8,128)S(1)} %get-tuple-element.18), channel_id=1, source_target_pairs={{0,12},{4,8},{8,4},{12,0},{1,13},{5,9},{9,5},{13,1},{2,14},{6,10},... | collective-permute-start | bytes 147464 | tf_op jit(solution)/shard_map/ppermute | solution.py:94
  54.6 3.9 %collective-permute-start.9 = (f32[48,128]{1,0:T(8,128)S(1)}, f32[48,128]{1,0:T(8,128)S(1)}, u32[]{:S(2)}, u32[]{:S(2)}) collective-permute-start(f32[48,128]{1,0:T(8,128)S(1)} %slice.29), channel_id=1, source_target_pairs={{0,2},{1,3},{2,0},{3,1},{4,6},{5,7},{6,4},{7,5},{8,10},{9,11},{10,... | collective-permute-start | bytes 73736 | tf_op jit(solution)/shard_map/ppermute | solution.py:102

commit v2 on v1

--- a/solution.py
+++ b/solution.py
@@ -3,6 +3,8 @@
 
 import jax
 import jax.numpy as jnp
+import ml_dtypes
+import numpy as np
 from jax import lax
 from jax.experimental import pallas as pl
 from jax.experimental.pallas import tpu as pltpu
@@ -15,10 +17,19 @@
 
 
 def dft_table(freqs, lags):
-    fvals = jnp.arange(freqs, dtype=jnp.float32)
-    tvals = jnp.arange(lags, dtype=jnp.float32) - lags // 2
-    phase = math.pi / freqs * fvals[:, None] * tvals[None, :]
-    return jnp.concatenate([jnp.cos(phase), -jnp.sin(phase)], 0) * (1.0 / math.sqrt(freqs))
+    fvals = np.arange(freqs, dtype=np.float32)
+    tvals = np.arange(lags, dtype=np.float32) - np.float32(lags // 2)
+    phase = (np.float32(math.pi / freqs) * fvals[:, None]) * tvals[None, :]
+    wave = np.exp(1j * phase.astype(np.float64))
+    parts = np.concatenate([wave.real, -wave.imag], 0).astype(np.float32)
+    return parts * np.float32(1.0 / math.sqrt(freqs))
+
+
+def split_table(freqs, lags):
+    table = dft_table(freqs, lags)
+    hi = table.astype(ml_dtypes.bfloat16)
+    lo = (table - hi.astype(np.float32)).astype(ml_dtypes.bfloat16)
+    return [jnp.asarray(t) for t in (hi, lo, hi.T.copy(), lo.T.copy())]
 
 
 def split(x):
@@ -30,22 +41,33 @@
     return jnp.dot(a, b, preferred_element_type=f32)
 
 
-def table_kernel(table, th, tl, bh, bl):
-    value = table[...]
-    th[...], tl[...] = split(value)
-    bh[...], bl[...] = split(value.T)
-
-
-def split_table(table):
-    size, lags = table.shape
-    shapes = [(size, lags), (size, lags), (lags, size), (lags, size)]
-    return pl.pallas_call(
-        table_kernel,
-        out_shape=[jax.ShapeDtypeStruct(s, bf16) for s in shapes],
+def stage_kernel(*refs):
+    count = len(refs) // 2
+    sources, (*kept, sems) = refs[:count], refs[count:]
+    copies = [pltpu.make_async_copy(s, k, sems.at[n]) for n, (s, k) in enumerate(zip(sources, kept))]
+    for copy in copies:
+        copy.start()
+    for copy in copies:
+        copy.wait()
+
+
+def stage(vectors, scalars):
+    arrays = list(vectors) + list(scalars)
+    shapes = [pltpu.VMEM(a.shape, a.dtype) for a in vectors]
+    shapes += [pltpu.SMEM(a.shape, a.dtype) for a in scalars]
+    kept = pl.pallas_call(
+        stage_kernel,
+        in_specs=[pl.BlockSpec(memory_space=pl.ANY)] * len(arrays),
+        out_specs=[pl.BlockSpec(memory_space=pltpu.VMEM)] * len(vectors)
+        + [pl.BlockSpec(memory_space=pltpu.SMEM)] * len(scalars),
+        out_shape=shapes,
+        scratch_shapes=[pltpu.SemaphoreType.DMA((len(arrays),))],
+        compiler_params=pltpu.CompilerParams(vmem_limit_bytes=58 * 2**20),
         cost_estimate=pl.CostEstimate(
-            flops=8 * size * lags, bytes_accessed=12 * size * lags, transcendentals=0
+            flops=0, bytes_accessed=2 * sum(a.size * a.dtype.itemsize for a in vectors), transcendentals=0
         ),
-    )(table)
+    )(*arrays)
+    return kept[: len(vectors)], kept[len(vectors) :]
 
 
 def bits_of(n):
@@ -74,9 +96,9 @@
     return [(i, i ^ k) for i in range(n)]
 
 
-def gather(piece, sta, band):
+def gather(piece, own, sta, band):
     got = {k: lax.ppermute(piece, "sta", pairs(sta, k)) for k in range(sta - 1, 0, -1)}
-    held = [piece] + [got[k] for k in range(1, sta)]
+    held = [own] + [got[k] for k in range(1, sta)]
     for bit in reversed(bits_of(band)):
         whole = jnp.concatenate(held, 0) if len(held) > 1 else held[0]
         held = [whole, lax.ppermute(whole, "band", pairs(band, bit))]
@@ -132,7 +154,7 @@
         re = slice(c * LANES, (c + 1) * LANES)
         im = slice(half + c * LANES, half + (c + 1) * LANES)
         bre, bim = ub[:, re], ub[:, im]
-        ares, aims = ua[pl.ds(p0, count), re], ua[pl.ds(p0, count), im]
+        ares, aims = ua[p0 : p0 + count, re], ua[p0 : p0 + count, im]
         for p in range(count):
             at = slice(p * tile, (p + 1) * tile)
             are, aim = ares[p : p + 1], aims[p : p + 1]
@@ -144,10 +166,7 @@
     return dot(xh[...], th[...]) + (dot(xl[...], th[...]) + dot(xh[...], tl[...]))
 
 
-def spectral_rows(lagged, seen, bh, bl):
-    misfit = lagged - seen
-    weighted = misfit + cubic_weight * misfit * misfit * misfit
-    wh, wl = split(weighted)
+def spectral_rows(wh, wl, bh, bl):
     return dot(wh, bh[...]) + (dot(wl, bh[...]) + dot(wh, bl[...]))
 
 
@@ -156,7 +175,7 @@
         re = slice(c * LANES, (c + 1) * LANES)
         im = slice(half + c * LANES, half + (c + 1) * LANES)
         bre, bim = ub[:, re], ub[:, im]
-        ares, aims = ua[pl.ds(p0, count), re], ua[pl.ds(p0, count), im]
+        ares, aims = ua[p0 : p0 + count, re], ua[p0 : p0 + count, im]
         cre, cim = cols[:, re], cols[:, im]
         rre, rim = [], []
         for p in range(count):
@@ -169,8 +188,8 @@
             cim = cim + (sre * aim - sim * are)
         cols[:, re] = cre
         cols[:, im] = cim
-        rows[pl.ds(p0, count), re] = jnp.concatenate(rre, 0)
-        rows[pl.ds(p0, count), im] = jnp.concatenate(rim, 0)
+        rows[p0 : p0 + count, re] = jnp.concatenate(rre, 0)
+        rows[p0 : p0 + count, im] = jnp.concatenate(rim, 0)
 
 
 def give_terms(tiles, place, me, rows, cols, blocked, outs, geometry, tile):
@@ -205,55 +224,65 @@
     half = th.shape[0] // 2
     lags = th.shape[1]
     if backward:
-        observed, refs = refs[0], refs[1:]
+        seen, refs = refs[0], refs[1:]
         if not forward:
             given, refs = refs[0], refs[1:]
         outs, refs = refs[:n_out], refs[n_out:]
     else:
         lagged_out, refs = refs[0], refs[1:]
-    blocked, ua, ub, xh, xl, spec, rows, cols = refs[:8]
+    blocked, ua, ub, rows, cols = refs[:5]
+    xh, xl, spec = refs[5:7], refs[7:9], refs[9:11]
     tile = ua.shape[0]
     if backward:
-        seen, sem = refs[8:]
-        fetch = pltpu.make_async_copy(observed.at[0], seen, sem)
-        fetch.start()
+        wh, wl = refs[11:]
     place_stations(held, place, me, blocked, geometry)
     load_block(blocked, tiles[0, 0], ua, tile, per)
     load_block(blocked, tiles[0, 1], ub, tile, per)
     if backward:
         cols[...] = jnp.zeros_like(cols)
-        fetch.wait()
-
-    def body(i, carry):
-        p0 = pl.multiple_of(i * step, step)
-        m0 = pl.multiple_of(i * (step * tile), step * tile)
-        if forward:
-            cross_rows(p0, step, ua, ub, xh, xl, tile, half)
-            lagged = lag_rows(xh, xl, th, tl)
+
+    steps = tile // step
+
+    def cross_step(i):
+        if forward and i < steps:
+            cross_rows(i * step, step, ua, ub, xh[i % 2], xl[i % 2], tile, half)
+
+    def lag_step(i):
+        span = slice(i * step * tile, (i + 1) * step * tile)
+        lagged = lag_rows(xh[i % 2], xl[i % 2], th, tl) if forward else given[span, :]
+        if backward:
+            misfit = lagged - seen[i * step : (i + 1) * step].reshape(step * tile, lags)
+            weighted = misfit + cubic_weight * misfit * misfit * misfit
+            wh[span, :], wl[span, :] = split(weighted)
         else:
-            lagged = given[pl.ds(m0, step * tile), :]
-        if not backward:
-            lagged_out[pl.ds(m0, step * tile), :] = lagged
-            return carry
-        look = seen[pl.ds(p0, step)].reshape(step * tile, lags)
-        spec[...] = spectral_rows(lagged, look, bh, bl)
-        adjoint_rows(p0, step, spec, ua, ub, rows, cols, tile, half)
-        return carry
-
-    lax.fori_loop(0, tile // step, body, 0)
+            lagged_out[span, :] = lagged
+
+    def spectral_step(i):
+        if i < steps:
+            span = slice(i * step * tile, (i + 1) * step * tile)
+            spec[i % 2][...] = spectral_rows(wh[span, :], wl[span, :], bh, bl)
+
+    cross_step(0)
+    for i in range(steps):
+        cross_step(i + 1)
+        lag_step(i)
+    if backward:
+        spectral_step(0)
+        for i in range(steps):
+            spectral_step(i + 1)
+            adjoint_rows(i * step, step, spec[i % 2], ua, ub, rows, cols, tile, half)
     if backward:
         give_terms(tiles, place, me, rows, cols, blocked, outs, geometry, tile)
 
 
-def tile_call(geometry, tiles, place, me, held, tables, observed, lagged=None, forward=True, backward=True):
+def tile_call(geometry, tiles, place, me, held, tables, seen, lagged=None, forward=True, backward=True):
     sta, band, rows, per = geometry
-    tile, lags = observed.shape[2], observed.shape[3]
+    tile, lags = seen.shape[1:]
     width = per * LANES
-    step = 8
+    step = 16
     count = place.shape[0]
     smem = pl.BlockSpec(memory_space=pltpu.SMEM)
     vmem = pl.BlockSpec(memory_space=pltpu.VMEM)
-    anys = pl.BlockSpec(memory_space=pl.ANY)
     args = [tiles, place, me, *held, *tables]
     specs = [smem] * 3 + [vmem] * (len(held) + 4)
     n_out = 2 if band > 1 else 1
@@ -261,20 +290,22 @@
         pltpu.VMEM((count * per, LANES), f32),
         pltpu.VMEM((tile, width), f32),
         pltpu.VMEM((tile, width), f32),
-        pltpu.VMEM((step * tile, width), bf16),
-        pltpu.VMEM((step * tile, width), bf16),
-        pltpu.VMEM((step * tile, width), f32),
         pltpu.VMEM((tile, width), f32),
         pltpu.VMEM((tile, width), f32),
     ]
-    if backward:
-        args.append(observed)
-        specs.append(anys)
+    scratch += [pltpu.VMEM((step * tile, width), bf16)] * 4
+    scratch += [pltpu.VMEM((step * tile, width), f32)] * 2
+    if backward:
+        args.append(seen)
+        specs.append(vmem)
         if not forward:
             args.append(lagged)
             specs.append(vmem)
         out_shape = [jax.ShapeDtypeStruct((count * per // n_out, LANES), f32)] * n_out
-        scratch += [pltpu.VMEM((tile, tile, lags), f32), pltpu.SemaphoreType.DMA]
+        scratch += [
+            pltpu.VMEM((tile * tile, lags), bf16),
+            pltpu.VMEM((tile * tile, lags), bf16),
+        ]
     else:
         out_shape = [jax.ShapeDtypeStruct((tile * tile, lags), f32)]
     pairs_count = tile * tile
@@ -298,15 +329,16 @@
     per = width // LANES
     geometry = (sta, band, rows, per)
     piece = spectra.reshape(rows * per, LANES)
-    held = gather(piece, sta, band)
     me = jnp.stack([lax.axis_index("sta"), lax.axis_index("band")]).astype(jnp.int32)
-    tables = split_table(dft_table(width // 2, observed.shape[3]))
+    tables = split_table(width // 2, observed.shape[3])
+    (own, seen, *tables), (tiles, place, me) = stage([piece, observed[0], *tables], [tiles, place, me])
+    held = gather(piece, own, sta, band)
     if src == 1:
-        parts = tile_call(geometry, tiles, place, me, held, tables, observed)
+        parts = tile_call(geometry, tiles, place, me, held, tables, seen)
     else:
-        (lagged,) = tile_call(geometry, tiles, place, me, held, tables, observed, backward=False)
+        (lagged,) = tile_call(geometry, tiles, place, me, held, tables, seen, backward=False)
         lagged = lax.psum(lagged, "src")
-        parts = tile_call(geometry, tiles, place, me, held, tables, observed, lagged, forward=False)
+        parts = tile_call(geometry, tiles, place, me, held, tables, seen, lagged, forward=False)
     return scatter_sum(parts, sta, band).reshape(spectra.shape)
 
 

time: 59.6 us -> 43.9 us (0.74)
  Pallas kernels: 21.3 us -> 15.2 us
  other arithmetic: 6.57 us -> 1.25 us
  local copies, waits for them, and re-layouts: 4.95 us -> 0.04 us
  waiting for transfers between devices: 12.4 us -> 14.6 us
  starting transfers between devices: 13.8 us -> 12.6 us
    pallas_call x1, Pallas kernels: 18.6 us -> 12.8 us  [tile_call(): pl.pallas_call(functools.partial(tile_kernel, geometry, len(held), n_out,...]
    unnamed x18 -> x4, local copies, waits for them, and re-layouts: 4.92 us -> 0.01 us
    cos x1 -> x0, other arithmetic: 2.96 us -> none  [dft_table(): jnp.cos(phase)]
    mul x2 -> x0, other arithmetic: 2.13 us -> none  [the longest x1 2.13 us: dft_table(): jnp.concatenate([jnp.cos(phase), -jnp.sin(phase)], 0)]
    ppermute x2, waiting for transfers between devices: 3.11 us -> 4.54 us  [gather(): held = [whole, lax.ppermute(whole, 'band', pairs(band, bit))]]
    ppermute x3, waiting for transfers between devices: 3.82 us -> 5.03 us  [scatter_sum(): lax.ppermute(total[k * each:(k + 1) * each], 'sta', pairs(sta, k))]
    ppermute x3, starting transfers between devices: 4.46 us -> 3.56 us  [scatter_sum(): lax.ppermute(total[k * each:(k + 1) * each], 'sta', pairs(sta, k))]
    concatenate x1, other arithmetic: 0.74 us -> 0.01 us  [gather(): whole = jnp.concatenate(held, 0) if len(held) > 1 else held[0]]
  transfers between devices with their start and end apart: 10 -> 10, of which waited for: 7 -> 8; matrix products, arithmetic and copies ran while one was open for 10% -> 1% of each run, Pallas kernels for 5% -> 5%
where the time goes in v2:
time: 43.9 us; the launch traced here: 43.7 us
  Pallas kernels  15.2 us (35%)
  waiting for transfers between devices  14.6 us (33%)
  starting transfers between devices  12.6 us (29%)
  other arithmetic  1.25 us (3%)
    pallas_call x1, Pallas kernels, tile_call(): pl.pallas_call(functools.partial(tile_kernel, geometry, len(held), n_out,...  12.8 us
    ppermute x3, starting transfers between devices, gather(): lax.ppermute(piece, 'sta', pairs(sta, k))  5.62 us
    ppermute x3, waiting for transfers between devices, scatter_sum(): lax.ppermute(total[k * each:(k + 1) * each], 'sta', pairs(sta, k))  5.03 us
    ppermute x2, waiting for transfers between devices, gather(): held = [whole, lax.ppermute(whole, 'band', pairs(band, bit))]  4.54 us
    ppermute x3, starting transfers between devices, scatter_sum(): lax.ppermute(total[k * each:(k + 1) * each], 'sta', pairs(sta, k))  3.56 us
    pallas_call x1, Pallas kernels, stage(): pl.pallas_call(stage_kernel, in_specs=[pl.BlockSpec(memory_space=pl.ANY)]...  2.34 us
    ppermute x1, waiting for transfers between devices, scatter_sum(): total = total[:half] + lax.ppermute(total[half:], 'band', pairs(band, bit))  2.34 us
    ppermute x2, starting transfers between devices, gather(): held = [whole, lax.ppermute(whole, 'band', pairs(band, bit))]  1.63 us
  transfers between devices with their start and end apart: 10, of which 8 were waited for; matrix products, arithmetic and copies ran while one was open for 1% of the time, Pallas kernels for 5%

profile of v2, /device:TPU:0, one launch (start us, length us, event | category | flops | bytes accessed | tf_op | source)
XLA Modules:
  0.0 43.7 jit_solution(15699927407250574391)
XLA Ops:
  0.0 5.0 %collective-permute-start.2 = (f32[48,128]{1,0:T(8,128)}, f32[48,128]{1,0:T(8,128)S(1)}, u32[]{:S(2)}, u32[]{:S(2)}) collective-permute-start(f32[48,128]{1,0:T(8,128)} %bitcast.6), channel_id=1, source_target_pairs={{0,12},{4,8},{8,4},{12,0},{1,13},{5,9},{9,5},{13,1},{2,14},{6,10},... | collective-permute-start | bytes 73736 | tf_op jit(solution)/shard_map/ppermute | solution.py:100
  5.0 0.0 collective-permute-start.1
  5.1 0.6 %collective-permute-start = (f32[48,128]{1,0:T(8,128)}, f32[48,128]{1,0:T(8,128)S(1)}, u32[]{:S(2)}, u32[]{:S(2)}) collective-permute-start(f32[48,128]{1,0:T(8,128)} %bitcast.8), channel_id=1, source_target_pairs={{0,4},{4,0},{8,12},{12,8},{1,5},{5,1},{9,13},{13,9},{2,6},{6,2},{1... | collective-permute-start | bytes 73736 | tf_op jit(solution)/shard_map/ppermute | solution.py:100
  5.6 0.6 %pad_add_fusion.refs_8_ = s32[2]{0:T(128)} fusion(s32[1]{0:T(128)} %bitcast.3, s32[1]{0:T(128)} %bitcast.2), kind=kLoop, calls=%fused_computation.10 | loop fusion | flops 2 | bytes 16 | tf_op jit(solution)/shard_map/stack | solution.py:332
  6.2 2.3 %shard_map.82 = (f32[48,128]{1,0:T(8,128)S(1)}, f32[48,48,256]{2,1,0:T(8,128)S(1)}, bf16[1024,256]{1,0:T(8,128)(2,1)S(1)}, bf16[1024,256]{1,0:T(8,128)(2,1)S(1)}...) custom-call(f32[48,128]{1,0:T(8,128)} %bitcast.9, ...), custom_call_target="tpu_custom_call" | custom-call | bytes 8962048 | tf_op jit(solution)/shard_map/pallas_call | solution.py:58
  8.6 0.0 collective-permute-done.2
  8.6 1.4 %collective-permute-done.1 = f32[48,128]{1,0:T(8,128)S(1)} collective-permute-done((f32[48,128]{1,0:T(8,128)}, f32[48,128]{1,0:T(8,128)S(1)}, u32[]{:S(2)}, u32[]{:S(2)}) %collective-permute-start.1) | collective-permute-done | bytes 24608 | tf_op jit(solution)/shard_map/ppermute | solution.py:100
  10.0 0.0 collective-permute-done
  10.0 1.6 %collective-permute-start.3 = (f32[192,128]{1,0:T(8,128)S(1)}, f32[192,128]{1,0:T(8,128)S(1)}, u32[]{:S(2)}, u32[]{:S(2)}) collective-permute-start(f32[192,128]{1,0:T(8,128)S(1)} %pad_maximum_fusion), channel_id=1, source_target_pairs={{0,2},{1,3},{2,0},{3,1},{4,6},{5,7},{6,4},{7,5},{8,10},{9,11},{10,... | collective-permute-start | bytes 294920 | tf_op jit(solution)/shard_map/ppermute | solution.py:104
  11.6 3.1 %collective-permute-done.3 = f32[192,128]{1,0:T(8,128)S(1)} collective-permute-done((f32[192,128]{1,0:T(8,128)S(1)}, f32[192,128]{1,0:T(8,128)S(1)}, u32[]{:S(2)}, u32[]{:S(2)}) %collective-permute-start.3) | collective-permute-done | bytes 98336 | tf_op jit(solution)/shard_map/ppermute | solution.py:104
  14.7 0.1 collective-permute-start.4
  14.8 1.4 %collective-permute-done.4.refs_1_ = f32[384,128]{1,0:T(8,128)S(1)} collective-permute-done((f32[384,128]{1,0:T(8,128)S(1)}, f32[384,128]{1,0:T(8,128)S(1)}, u32[]{:S(2)}, u32[]{:S(2)}) %collective-permute-start.4) | collective-permute-done | bytes 196640 | tf_op jit(solution)/shard_map/ppermute | solution.py:104
  16.2 12.8 %shard_map.83 = (f32[384,128]{1,0:T(8,128)S(1)}, f32[384,128]{1,0:T(8,128)S(1)}) custom-call(s32[1,2]{1,0:T(1,128)S(4)} %get-tuple-element.16.tiles, s32[96]{0:T(128)S(4)} %get-tuple-element.17.place, s32[2]{0:T(128)S(4)} %get-tuple-element.18.me, f32[384,128]{1,0:T(8,128)S(1)} %constant_dynamic-update-slice_fusion.refs_0_, ...), custom_call_target="tpu_custom_call" | custom-call | flops 7247757312 | bytes 9437184 | tf_op jit(solution)/shard_map/pallas_call | solution.py:312
  29.0 0.2 collective-permute-start.5
  29.2 1.3 %collective-permute-done.5 = f32[384,128]{1,0:T(8,128)S(1)} collective-permute-done((f32[384,128]{1,0:T(8,128)S(1)}, f32[384,128]{1,0:T(8,128)S(1)}, u32[]{:S(2)}, u32[]{:S(2)}) %collective-permute-start.5) | collective-permute-done | bytes 196640 | tf_op jit(solution)/shard_map/ppermute | solution.py:112
  30.6 0.1 collective-permute-start.6
  30.7 3.4 %collective-permute-start.8 = (f32[96,128]{1,0:T(8,128)S(1)}, f32[96,128]{1,0:T(8,128)S(1)}, u32[]{:S(2)}, u32[]{:S(2)}) collective-permute-start(f32[96,128]{1,0:T(8,128)S(1)} %get-tuple-element.28), channel_id=1, source_target_pairs={{0,12},{4,8},{8,4},{12,0},{1,13},{5,9},{9,5},{13,1},{2,14},{6,10},... | collective-permute-start | bytes 147464 | tf_op jit(solution)/shard_map/ppermute | solution.py:116
  34.2 0.0 collective-permute-start.7
  34.2 0.6 %collective-permute-done.6 = f32[96,128]{1,0:T(8,128)S(1)} collective-permute-done((f32[96,128]{1,0:T(8,128)S(1)}, f32[96,128]{1,0:T(8,128)S(1)}, u32[]{:S(2)}, u32[]{:S(2)}) %collective-permute-start.6) | collective-permute-done | bytes 49184 | tf_op jit(solution)/shard_map/ppermute | solution.py:116
  34.8 2.4 %collective-permute-done.8 = f32[96,128]{1,0:T(8,128)S(1)} collective-permute-done((f32[96,128]{1,0:T(8,128)S(1)}, f32[96,128]{1,0:T(8,128)S(1)}, u32[]{:S(2)}, u32[]{:S(2)}) %collective-permute-start.8) | collective-permute-done | bytes 49184 | tf_op jit(solution)/shard_map/ppermute | solution.py:116
  37.2 2.0 %collective-permute-done.7 = f32[96,128]{1,0:T(8,128)S(1)} collective-permute-done((f32[96,128]{1,0:T(8,128)S(1)}, f32[96,128]{1,0:T(8,128)S(1)}, u32[]{:S(2)}, u32[]{:S(2)}) %collective-permute-start.7) | collective-permute-done | bytes 49184 | tf_op jit(solution)/shard_map/ppermute | solution.py:116
  39.2 1.6 %collective-permute-start.9 = (f32[48,128]{1,0:T(8,128)S(1)}, f32[48,128]{1,0:T(8,128)S(1)}, u32[]{:S(2)}, u32[]{:S(2)}) collective-permute-start(f32[48,128]{1,0:T(8,128)S(1)} %slice.29), channel_id=1, source_target_pairs={{0,2},{1,3},{2,0},{3,1},{4,6},{5,7},{6,4},{7,5},{8,10},{9,11},{10,... | collective-permute-start | bytes 73736 | tf_op jit(solution)/shard_map/ppermute | solution.py:124
  40.8 2.3 %collective-permute-done.9 = f32[48,128]{1,0:T(8,128)S(1)} collective-permute-done((f32[48,128]{1,0:T(8,128)S(1)}, f32[48,128]{1,0:T(8,128)S(1)}, u32[]{:S(2)}, u32[]{:S(2)}) %collective-permute-start.9) | collective-permute-done | bytes 24608 | tf_op jit(solution)/shard_map/ppermute | solution.py:124
  43.1 0.6 %slice_add_fusion.1 = f32[48,128]{1,0:T(8,128)} fusion(f32[48,128]{1,0:T(8,128)S(1)} %collective-permute-done.9, f32[96,128]{1,0:T(8,128)S(1)} %fusion.1), kind=kLoop, calls=%fused_computation.4 | loop fusion | flops 6144 | bytes 73728 | tf_op jit(solution)/shard_map/add | solution.py:124
  (10 shorter events, 0.1 us)
Async XLA Ops:
  0.0 8.6 %collective-permute-start.2 = (f32[48,128]{1,0:T(8,128)}, f32[48,128]{1,0:T(8,128)S(1)}, u32[]{:S(2)}, u32[]{:S(2)}) collective-permute-start(f32[48,128]{1,0:T(8,128)} %bitcast.6), channel_id=1, source_target_pairs={{0,12},{4,8},{8,4},{12,0},{1,13},{5,9},{9,5},{13,1},{2,14},{6,10},... | collective-permute-start | bytes 73736 | tf_op jit(solution)/shard_map/ppermute | solution.py:100
  5.0 4.9 %collective-permute-start.1 = (f32[48,128]{1,0:T(8,128)}, f32[48,128]{1,0:T(8,128)S(1)}, u32[]{:S(2)}, u32[]{:S(2)}) collective-permute-start(f32[48,128]{1,0:T(8,128)} %bitcast.7), channel_id=1, source_target_pairs={{0,8},{4,12},{8,0},{12,4},{1,9},{5,13},{9,1},{13,5},{2,10},{6,14},... | collective-permute-start | bytes 73736 | tf_op jit(solution)/shard_map/ppermute | solution.py:100
  5.1 4.9 %collective-permute-start = (f32[48,128]{1,0:T(8,128)}, f32[48,128]{1,0:T(8,128)S(1)}, u32[]{:S(2)}, u32[]{:S(2)}) collective-permute-start(f32[48,128]{1,0:T(8,128)} %bitcast.8), channel_id=1, source_target_pairs={{0,4},{4,0},{8,12},{12,8},{1,5},{5,1},{9,13},{13,9},{2,6},{6,2},{1... | collective-permute-start | bytes 73736 | tf_op jit(solution)/shard_map/ppermute | solution.py:100
  10.0 4.7 %collective-permute-start.3 = (f32[192,128]{1,0:T(8,128)S(1)}, f32[192,128]{1,0:T(8,128)S(1)}, u32[]{:S(2)}, u32[]{:S(2)}) collective-permute-start(f32[192,128]{1,0:T(8,128)S(1)} %pad_maximum_fusion), channel_id=1, source_target_pairs={{0,2},{1,3},{2,0},{3,1},{4,6},{5,7},{6,4},{7,5},{8,10},{9,11},{10,... | collective-permute-start | bytes 294920 | tf_op jit(solution)/shard_map/ppermute | solution.py:104
  14.7 1.5 %collective-permute-start.4 = (f32[384,128]{1,0:T(8,128)S(1)}, f32[384,128]{1,0:T(8,128)S(1)}, u32[]{:S(2)}, u32[]{:S(2)}) collective-permute-start(f32[384,128]{1,0:T(8,128)S(1)} %constant_dynamic-update-slice_fusion.refs_0_), channel_id=1, source_target_pairs={{0,1},{1,0},{2,3},{3,2},{4,5},{5,4},{6,7},{7,6},{8,9},{9,8},{10,11... | collective-permute-start | bytes 589832 | tf_op jit(solution)/shard_map/ppermute | solution.py:104
  29.0 1.5 %collective-permute-start.5 = (f32[384,128]{1,0:T(8,128)S(1)}, f32[384,128]{1,0:T(8,128)S(1)}, u32[]{:S(2)}, u32[]{:S(2)}) collective-permute-start(f32[384,128]{1,0:T(8,128)S(1)} %get-tuple-element.26), channel_id=1, source_target_pairs={{0,1},{1,0},{2,3},{3,2},{4,5},{5,4},{6,7},{7,6},{8,9},{9,8},{10,11... | collective-permute-start | bytes 589832 | tf_op jit(solution)/shard_map/ppermute | solution.py:112
  30.6 4.2 %collective-permute-start.6 = (f32[96,128]{1,0:T(8,128)S(1)}, f32[96,128]{1,0:T(8,128)S(1)}, u32[]{:S(2)}, u32[]{:S(2)}) collective-permute-start(f32[96,128]{1,0:T(8,128)S(1)} %get-tuple-element.27), channel_id=1, source_target_pairs={{0,4},{4,0},{8,12},{12,8},{1,5},{5,1},{9,13},{13,9},{2,6},{6,2},{1... | collective-permute-start | bytes 147464 | tf_op jit(solution)/shard_map/ppermute | solution.py:116
  30.7 6.4 %collective-permute-start.8 = (f32[96,128]{1,0:T(8,128)S(1)}, f32[96,128]{1,0:T(8,128)S(1)}, u32[]{:S(2)}, u32[]{:S(2)}) collective-permute-start(f32[96,128]{1,0:T(8,128)S(1)} %get-tuple-element.28), channel_id=1, source_target_pairs={{0,12},{4,8},{8,4},{12,0},{1,13},{5,9},{9,5},{13,1},{2,14},{6,10},... | collective-permute-start | bytes 147464 | tf_op jit(solution)/shard_map/ppermute | solution.py:116
  34.2 5.0 %collective-permute-start.7 = (f32[96,128]{1,0:T(8,128)S(1)}, f32[96,128]{1,0:T(8,128)S(1)}, u32[]{:S(2)}, u32[]{:S(2)}) collective-permute-start(f32[96,128]{1,0:T(8,128)S(1)} %get-tuple-element.29), channel_id=1, source_target_pairs={{0,8},{4,12},{8,0},{12,4},{1,9},{5,13},{9,1},{13,5},{2,10},{6,14},... | collective-permute-start | bytes 147464 | tf_op jit(solution)/shard_map/ppermute | solution.py:116
  39.2 3.9 %collective-permute-start.9 = (f32[48,128]{1,0:T(8,128)S(1)}, f32[48,128]{1,0:T(8,128)S(1)}, u32[]{:S(2)}, u32[]{:S(2)}) collective-permute-start(f32[48,128]{1,0:T(8,128)S(1)} %slice.29), channel_id=1, source_target_pairs={{0,2},{1,3},{2,0},{3,1},{4,6},{5,7},{6,4},{7,5},{8,10},{9,11},{10,... | collective-permute-start | bytes 73736 | tf_op jit(solution)/shard_map/ppermute | solution.py:124

commit v3 on v2

--- a/solution.py
+++ b/solution.py
@@ -98,10 +98,9 @@
 
 def gather(piece, own, sta, band):
     got = {k: lax.ppermute(piece, "sta", pairs(sta, k)) for k in range(sta - 1, 0, -1)}
-    held = [own] + [got[k] for k in range(1, sta)]
+    held = [jnp.concatenate([own] + [got[k] for k in range(1, sta)], 0)]
     for bit in reversed(bits_of(band)):
-        whole = jnp.concatenate(held, 0) if len(held) > 1 else held[0]
-        held = [whole, lax.ppermute(whole, "band", pairs(band, bit))]
+        held = held + [lax.ppermute(one, "band", pairs(band, bit)) for one in held]
     return held
 
 
@@ -149,8 +148,8 @@
         out[:, j * LANES : (j + 1) * LANES] = view[pl.ds(j, tile, stride=per), :]
 
 
-def cross_rows(p0, count, ua, ub, xh, xl, tile, half):
-    for c in range(half // LANES):
+def cross_rows(chunks, p0, count, ua, ub, xh, xl, tile, half):
+    for c in chunks:
         re = slice(c * LANES, (c + 1) * LANES)
         im = slice(half + c * LANES, half + (c + 1) * LANES)
         bre, bim = ub[:, re], ub[:, im]
@@ -162,16 +161,23 @@
             xh[at, im], xl[at, im] = split(aim * bre - are * bim)
 
 
-def lag_rows(xh, xl, th, tl):
-    return dot(xh[...], th[...]) + (dot(xl[...], th[...]) + dot(xh[...], tl[...]))
-
-
-def spectral_rows(wh, wl, bh, bl):
-    return dot(wh, bh[...]) + (dot(wl, bh[...]) + dot(wh, bl[...]))
-
-
-def adjoint_rows(p0, count, spec, ua, ub, rows, cols, tile, half):
-    for c in range(half // LANES):
+def lag_part(c, xh, xl, th, tl, half):
+    re = slice(c * LANES, (c + 1) * LANES)
+    im = slice(half + c * LANES, half + (c + 1) * LANES)
+    left = [x[:, at] for x in (xh, xl, xh) for at in (re, im)]
+    right = [t[at, :] for t in (th, th, tl) for at in (re, im)]
+    return dot(jnp.concatenate(left, 1), jnp.concatenate(right, 0))
+
+
+def spectral_part(c, chunks, wh, wl, bh, bl):
+    size = bh.shape[1] // chunks
+    at = slice(c * size, (c + 1) * size)
+    left = jnp.concatenate([wh, wl, wh], 1)
+    return at, dot(left, jnp.concatenate([bh[:, at], bh[:, at], bl[:, at]], 0))
+
+
+def adjoint_rows(chunks, p0, count, spec, ua, ub, rows, cols, tile, half):
+    for c in chunks:
         re = slice(c * LANES, (c + 1) * LANES)
         im = slice(half + c * LANES, half + (c + 1) * LANES)
         bre, bim = ub[:, re], ub[:, im]
@@ -242,14 +248,14 @@
         cols[...] = jnp.zeros_like(cols)
 
     steps = tile // step
-
-    def cross_step(i):
+    chunks = half // LANES
+
+    def cross_step(i, c):
         if forward and i < steps:
-            cross_rows(i * step, step, ua, ub, xh[i % 2], xl[i % 2], tile, half)
-
-    def lag_step(i):
+            cross_rows(c, i * step, step, ua, ub, xh[i % 2], xl[i % 2], tile, half)
+
+    def weigh_step(i, lagged):
         span = slice(i * step * tile, (i + 1) * step * tile)
-        lagged = lag_rows(xh[i % 2], xl[i % 2], th, tl) if forward else given[span, :]
         if backward:
             misfit = lagged - seen[i * step : (i + 1) * step].reshape(step * tile, lags)
             weighted = misfit + cubic_weight * misfit * misfit * misfit
@@ -257,20 +263,30 @@
         else:
             lagged_out[span, :] = lagged
 
-    def spectral_step(i):
+    def spectral_step(i, c):
         if i < steps:
             span = slice(i * step * tile, (i + 1) * step * tile)
-            spec[i % 2][...] = spectral_rows(wh[span, :], wl[span, :], bh, bl)
-
-    cross_step(0)
+            at, value = spectral_part(c, chunks, wh[span, :], wl[span, :], bh, bl)
+            spec[i % 2][:, at] = value
+
+    cross_step(0, range(chunks))
     for i in range(steps):
-        cross_step(i + 1)
-        lag_step(i)
-    if backward:
-        spectral_step(0)
+        if forward:
+            lagged = None
+            for c in range(chunks):
+                part = lag_part(c, xh[i % 2], xl[i % 2], th, tl, half)
+                lagged = part if lagged is None else lagged + part
+                cross_step(i + 1, [c])
+        else:
+            lagged = given[i * step * tile : (i + 1) * step * tile, :]
+        weigh_step(i, lagged)
+    if backward:
+        for c in range(chunks):
+            spectral_step(0, c)
         for i in range(steps):
-            spectral_step(i + 1)
-            adjoint_rows(i * step, step, spec[i % 2], ua, ub, rows, cols, tile, half)
+            for c in range(chunks):
+                spectral_step(i + 1, c)
+                adjoint_rows([c], i * step, step, spec[i % 2], ua, ub, rows, cols, tile, half)
     if backward:
         give_terms(tiles, place, me, rows, cols, blocked, outs, geometry, tile)
 

time: 43.9 us -> 42.9 us (0.977)
  Pallas kernels: 15.2 us -> 14.4 us
    pallas_call x1, Pallas kernels: 12.8 us -> 12.1 us  [tile_call(): pl.pallas_call(functools.partial(tile_kernel, geometry, len(held), n_out,...]
    ppermute x2 -> x3, waiting for transfers between devices: 4.54 us -> 4.42 us  [gather(): held = held + [lax.ppermute(one, 'band', pairs(band, bit)) for one in held]]
    ppermute x2 -> x3, starting transfers between devices: 1.63 us -> 1.56 us  [gather(): held = held + [lax.ppermute(one, 'band', pairs(band, bit)) for one in held]]
  transfers between devices with their start and end apart: 10 -> 11, of which waited for: 8 -> 9; matrix products, arithmetic and copies ran while one was open for 1% -> 1% of each run, Pallas kernels for 5% -> 5%
where the time goes in v3:
time: 42.9 us; the launch traced here: 42.8 us
  waiting for transfers between devices  14.5 us (34%)
  Pallas kernels  14.4 us (34%)
  starting transfers between devices  12.5 us (29%)
  other arithmetic  1.27 us (3%)
    pallas_call x1, Pallas kernels, tile_call(): pl.pallas_call(functools.partial(tile_kernel, geometry, len(held), n_out,...  12.1 us
    ppermute x3, starting transfers between devices, gather(): lax.ppermute(piece, 'sta', pairs(sta, k))  5.62 us
    ppermute x3, waiting for transfers between devices, scatter_sum(): lax.ppermute(total[k * each:(k + 1) * each], 'sta', pairs(sta, k))  5.06 us
    ppermute x3, waiting for transfers between devices, gather(): held = held + [lax.ppermute(one, 'band', pairs(band, bit)) for one in held]  4.42 us
    ppermute x3, starting transfers between devices, scatter_sum(): lax.ppermute(total[k * each:(k + 1) * each], 'sta', pairs(sta, k))  3.59 us
    pallas_call x1, Pallas kernels, stage(): pl.pallas_call(stage_kernel, in_specs=[pl.BlockSpec(memory_space=pl.ANY)]...  2.34 us
    ppermute x1, waiting for transfers between devices, scatter_sum(): total = total[:half] + lax.ppermute(total[half:], 'band', pairs(band, bit))  2.34 us
    ppermute x3, starting transfers between devices, gather(): held = held + [lax.ppermute(one, 'band', pairs(band, bit)) for one in held]  1.56 us
  transfers between devices with their start and end apart: 11, of which 9 were waited for; matrix products, arithmetic and copies ran while one was open for 1% of the time, Pallas kernels for 5%

profile of v3, /device:TPU:0, one launch (start us, length us, event | category | flops | bytes accessed | tf_op | source)
XLA Modules:
  0.0 42.8 jit_solution(10883712775792491449)
XLA Ops:
  0.0 5.0 %collective-permute-start.2 = (f32[48,128]{1,0:T(8,128)}, f32[48,128]{1,0:T(8,128)S(1)}, u32[]{:S(2)}, u32[]{:S(2)}) collective-permute-start(f32[48,128]{1,0:T(8,128)} %bitcast.6), channel_id=1, source_target_pairs={{0,12},{4,8},{8,4},{12,0},{1,13},{5,9},{9,5},{13,1},{2,14},{6,10},... | collective-permute-start | bytes 73736 | tf_op jit(solution)/shard_map/ppermute | solution.py:100
  5.0 0.0 collective-permute-start.1
  5.1 0.6 %collective-permute-start = (f32[48,128]{1,0:T(8,128)}, f32[48,128]{1,0:T(8,128)S(1)}, u32[]{:S(2)}, u32[]{:S(2)}) collective-permute-start(f32[48,128]{1,0:T(8,128)} %bitcast.8), channel_id=1, source_target_pairs={{0,4},{4,0},{8,12},{12,8},{1,5},{5,1},{9,13},{13,9},{2,6},{6,2},{1... | collective-permute-start | bytes 73736 | tf_op jit(solution)/shard_map/ppermute | solution.py:100
  5.6 0.6 %pad_add_fusion.refs_8_ = s32[2]{0:T(128)} fusion(s32[1]{0:T(128)} %bitcast.3, s32[1]{0:T(128)} %bitcast.2), kind=kLoop, calls=%fused_computation.8 | loop fusion | flops 2 | bytes 16 | tf_op jit(solution)/shard_map/stack | solution.py:348
  6.2 2.3 %shard_map.82 = (f32[48,128]{1,0:T(8,128)S(1)}, f32[48,48,256]{2,1,0:T(8,128)S(1)}, bf16[1024,256]{1,0:T(8,128)(2,1)S(1)}, bf16[1024,256]{1,0:T(8,128)(2,1)S(1)}...) custom-call(f32[48,128]{1,0:T(8,128)} %bitcast.9, ...), custom_call_target="tpu_custom_call" | custom-call | bytes 8962048 | tf_op jit(solution)/shard_map/pallas_call | solution.py:58
  8.6 0.5 %collective-permute-done = f32[48,128]{1,0:T(8,128)S(1)} collective-permute-done((f32[48,128]{1,0:T(8,128)}, f32[48,128]{1,0:T(8,128)S(1)}, u32[]{:S(2)}, u32[]{:S(2)}) %collective-permute-start) | collective-permute-done | bytes 24608 | tf_op jit(solution)/shard_map/ppermute | solution.py:100
  9.1 0.9 %collective-permute-done.1 = f32[48,128]{1,0:T(8,128)S(1)} collective-permute-done((f32[48,128]{1,0:T(8,128)}, f32[48,128]{1,0:T(8,128)S(1)}, u32[]{:S(2)}, u32[]{:S(2)}) %collective-permute-start.1) | collective-permute-done | bytes 24608 | tf_op jit(solution)/shard_map/ppermute | solution.py:100
  10.0 0.0 collective-permute-done.2
  10.0 1.6 %collective-permute-start.3 = (f32[192,128]{1,0:T(8,128)S(1)}, f32[192,128]{1,0:T(8,128)S(1)}, u32[]{:S(2)}, u32[]{:S(2)}) collective-permute-start(f32[192,128]{1,0:T(8,128)S(1)} %constant_dynamic-update-slice_fusion.refs_0_), channel_id=1, source_target_pairs={{0,2},{1,3},{2,0},{3,1},{4,6},{5,7},{6,4},{7,5},{8,10},{9,11},{10,... | collective-permute-start | bytes 294920 | tf_op jit(solution)/shard_map/ppermute | solution.py:103
  11.6 0.0 collective-permute-start.4
  11.6 3.1 %collective-permute-done.3.refs_1_ = f32[192,128]{1,0:T(8,128)S(1)} collective-permute-done((f32[192,128]{1,0:T(8,128)S(1)}, f32[192,128]{1,0:T(8,128)S(1)}, u32[]{:S(2)}, u32[]{:S(2)}) %collective-permute-start.3) | collective-permute-done | bytes 98336 | tf_op jit(solution)/shard_map/ppermute | solution.py:103
  14.7 0.0 collective-permute-start.5
  14.7 0.0 collective-permute-done.4.refs_2_
  14.7 1.3 %collective-permute-done.5.refs_3_ = f32[192,128]{1,0:T(8,128)S(1)} collective-permute-done((f32[192,128]{1,0:T(8,128)S(1)}, f32[192,128]{1,0:T(8,128)S(1)}, u32[]{:S(2)}, u32[]{:S(2)}) %collective-permute-start.5) | collective-permute-done | bytes 98336 | tf_op jit(solution)/shard_map/ppermute | solution.py:103
  16.0 12.1 %shard_map.83 = (f32[384,128]{1,0:T(8,128)S(1)}, f32[384,128]{1,0:T(8,128)S(1)}) custom-call(s32[1,2]{1,0:T(1,128)S(4)} %get-tuple-element.16.tiles, s32[96]{0:T(128)S(4)} %get-tuple-element.17.place, s32[2]{0:T(128)S(4)} %get-tuple-element.18.me, f32[192,128]{1,0:T(8,128)S(1)} %constant_dynamic-update-slice_fusion.refs_0_, ...), custom_call_target="tpu_custom_call" | custom-call | flops 7247757312 | bytes 9437184 | tf_op jit(solution)/shard_map/pallas_call | solution.py:328
  28.1 0.2 collective-permute-start.6
  28.3 1.3 %collective-permute-done.6 = f32[384,128]{1,0:T(8,128)S(1)} collective-permute-done((f32[384,128]{1,0:T(8,128)S(1)}, f32[384,128]{1,0:T(8,128)S(1)}, u32[]{:S(2)}, u32[]{:S(2)}) %collective-permute-start.6) | collective-permute-done | bytes 196640 | tf_op jit(solution)/shard_map/ppermute | solution.py:111
  29.6 0.2 collective-permute-start.7
  29.8 3.4 %collective-permute-start.9 = (f32[96,128]{1,0:T(8,128)S(1)}, f32[96,128]{1,0:T(8,128)S(1)}, u32[]{:S(2)}, u32[]{:S(2)}) collective-permute-start(f32[96,128]{1,0:T(8,128)S(1)} %get-tuple-element.28), channel_id=1, source_target_pairs={{0,12},{4,8},{8,4},{12,0},{1,13},{5,9},{9,5},{13,1},{2,14},{6,10},... | collective-permute-start | bytes 147464 | tf_op jit(solution)/shard_map/ppermute | solution.py:115
  33.2 0.0 collective-permute-start.8
  33.2 0.6 %collective-permute-done.7 = f32[96,128]{1,0:T(8,128)S(1)} collective-permute-done((f32[96,128]{1,0:T(8,128)S(1)}, f32[96,128]{1,0:T(8,128)S(1)}, u32[]{:S(2)}, u32[]{:S(2)}) %collective-permute-start.7) | collective-permute-done | bytes 49184 | tf_op jit(solution)/shard_map/ppermute | solution.py:115
  33.8 2.4 %collective-permute-done.9 = f32[96,128]{1,0:T(8,128)S(1)} collective-permute-done((f32[96,128]{1,0:T(8,128)S(1)}, f32[96,128]{1,0:T(8,128)S(1)}, u32[]{:S(2)}, u32[]{:S(2)}) %collective-permute-start.9) | collective-permute-done | bytes 49184 | tf_op jit(solution)/shard_map/ppermute | solution.py:115
  36.2 2.0 %collective-permute-done.8 = f32[96,128]{1,0:T(8,128)S(1)} collective-permute-done((f32[96,128]{1,0:T(8,128)S(1)}, f32[96,128]{1,0:T(8,128)S(1)}, u32[]{:S(2)}, u32[]{:S(2)}) %collective-permute-start.8) | collective-permute-done | bytes 49184 | tf_op jit(solution)/shard_map/ppermute | solution.py:115
  38.3 1.6 %collective-permute-start.10 = (f32[48,128]{1,0:T(8,128)S(1)}, f32[48,128]{1,0:T(8,128)S(1)}, u32[]{:S(2)}, u32[]{:S(2)}) collective-permute-start(f32[48,128]{1,0:T(8,128)S(1)} %slice.29), channel_id=1, source_target_pairs={{0,2},{1,3},{2,0},{3,1},{4,6},{5,7},{6,4},{7,5},{8,10},{9,11},{10,... | collective-permute-start | bytes 73736 | tf_op jit(solution)/shard_map/ppermute | solution.py:123
  39.8 2.3 %collective-permute-done.10 = f32[48,128]{1,0:T(8,128)S(1)} collective-permute-done((f32[48,128]{1,0:T(8,128)S(1)}, f32[48,128]{1,0:T(8,128)S(1)}, u32[]{:S(2)}, u32[]{:S(2)}) %collective-permute-start.10) | collective-permute-done | bytes 24608 | tf_op jit(solution)/shard_map/ppermute | solution.py:123
  42.2 0.6 %slice_add_fusion.1 = f32[48,128]{1,0:T(8,128)} fusion(f32[48,128]{1,0:T(8,128)S(1)} %collective-permute-done.10, f32[96,128]{1,0:T(8,128)S(1)} %fusion.1), kind=kLoop, calls=%fused_computation.3 | loop fusion | flops 6144 | bytes 73728 | tf_op jit(solution)/shard_map/add | solution.py:123
  (8 shorter events, 0.1 us)
Async XLA Ops:
  0.0 10.0 %collective-permute-start.2 = (f32[48,128]{1,0:T(8,128)}, f32[48,128]{1,0:T(8,128)S(1)}, u32[]{:S(2)}, u32[]{:S(2)}) collective-permute-start(f32[48,128]{1,0:T(8,128)} %bitcast.6), channel_id=1, source_target_pairs={{0,12},{4,8},{8,4},{12,0},{1,13},{5,9},{9,5},{13,1},{2,14},{6,10},... | collective-permute-start | bytes 73736 | tf_op jit(solution)/shard_map/ppermute | solution.py:100
  5.0 4.9 %collective-permute-start.1 = (f32[48,128]{1,0:T(8,128)}, f32[48,128]{1,0:T(8,128)S(1)}, u32[]{:S(2)}, u32[]{:S(2)}) collective-permute-start(f32[48,128]{1,0:T(8,128)} %bitcast.7), channel_id=1, source_target_pairs={{0,8},{4,12},{8,0},{12,4},{1,9},{5,13},{9,1},{13,5},{2,10},{6,14},... | collective-permute-start | bytes 73736 | tf_op jit(solution)/shard_map/ppermute | solution.py:100
  5.1 4.0 %collective-permute-start = (f32[48,128]{1,0:T(8,128)}, f32[48,128]{1,0:T(8,128)S(1)}, u32[]{:S(2)}, u32[]{:S(2)}) collective-permute-start(f32[48,128]{1,0:T(8,128)} %bitcast.8), channel_id=1, source_target_pairs={{0,4},{4,0},{8,12},{12,8},{1,5},{5,1},{9,13},{13,9},{2,6},{6,2},{1... | collective-permute-start | bytes 73736 | tf_op jit(solution)/shard_map/ppermute | solution.py:100
  10.0 4.7 %collective-permute-start.3 = (f32[192,128]{1,0:T(8,128)S(1)}, f32[192,128]{1,0:T(8,128)S(1)}, u32[]{:S(2)}, u32[]{:S(2)}) collective-permute-start(f32[192,128]{1,0:T(8,128)S(1)} %constant_dynamic-update-slice_fusion.refs_0_), channel_id=1, source_target_pairs={{0,2},{1,3},{2,0},{3,1},{4,6},{5,7},{6,4},{7,5},{8,10},{9,11},{10,... | collective-permute-start | bytes 294920 | tf_op jit(solution)/shard_map/ppermute | solution.py:103
  11.6 3.1 %collective-permute-start.4 = (f32[192,128]{1,0:T(8,128)S(1)}, f32[192,128]{1,0:T(8,128)S(1)}, u32[]{:S(2)}, u32[]{:S(2)}) collective-permute-start(f32[192,128]{1,0:T(8,128)S(1)} %constant_dynamic-update-slice_fusion.refs_0_), channel_id=1, source_target_pairs={{0,1},{1,0},{2,3},{3,2},{4,5},{5,4},{6,7},{7,6},{8,9},{9,8},{10,11... | collective-permute-start | bytes 294920 | tf_op jit(solution)/shard_map/ppermute | solution.py:103
  14.7 1.3 %collective-permute-start.5 = (f32[192,128]{1,0:T(8,128)S(1)}, f32[192,128]{1,0:T(8,128)S(1)}, u32[]{:S(2)}, u32[]{:S(2)}) collective-permute-start(f32[192,128]{1,0:T(8,128)S(1)} %collective-permute-done.3.refs_1_), channel_id=1, source_target_pairs={{0,1},{1,0},{2,3},{3,2},{4,5},{5,4},{6,7},{7,6},{8,9},{9,8},{10,11... | collective-permute-start | bytes 294920 | tf_op jit(solution)/shard_map/ppermute | solution.py:103
  28.1 1.5 %collective-permute-start.6 = (f32[384,128]{1,0:T(8,128)S(1)}, f32[384,128]{1,0:T(8,128)S(1)}, u32[]{:S(2)}, u32[]{:S(2)}) collective-permute-start(f32[384,128]{1,0:T(8,128)S(1)} %get-tuple-element.26), channel_id=1, source_target_pairs={{0,1},{1,0},{2,3},{3,2},{4,5},{5,4},{6,7},{7,6},{8,9},{9,8},{10,11... | collective-permute-start | bytes 589832 | tf_op jit(solution)/shard_map/ppermute | solution.py:111
  29.6 4.2 %collective-permute-start.7 = (f32[96,128]{1,0:T(8,128)S(1)}, f32[96,128]{1,0:T(8,128)S(1)}, u32[]{:S(2)}, u32[]{:S(2)}) collective-permute-start(f32[96,128]{1,0:T(8,128)S(1)} %get-tuple-element.27), channel_id=1, source_target_pairs={{0,4},{4,0},{8,12},{12,8},{1,5},{5,1},{9,13},{13,9},{2,6},{6,2},{1... | collective-permute-start | bytes 147464 | tf_op jit(solution)/shard_map/ppermute | solution.py:115
  29.8 6.4 %collective-permute-start.9 = (f32[96,128]{1,0:T(8,128)S(1)}, f32[96,128]{1,0:T(8,128)S(1)}, u32[]{:S(2)}, u32[]{:S(2)}) collective-permute-start(f32[96,128]{1,0:T(8,128)S(1)} %get-tuple-element.28), channel_id=1, source_target_pairs={{0,12},{4,8},{8,4},{12,0},{1,13},{5,9},{9,5},{13,1},{2,14},{6,10},... | collective-permute-start | bytes 147464 | tf_op jit(solution)/shard_map/ppermute | solution.py:115
  33.2 5.1 %collective-permute-start.8 = (f32[96,128]{1,0:T(8,128)S(1)}, f32[96,128]{1,0:T(8,128)S(1)}, u32[]{:S(2)}, u32[]{:S(2)}) collective-permute-start(f32[96,128]{1,0:T(8,128)S(1)} %get-tuple-element.29), channel_id=1, source_target_pairs={{0,8},{4,12},{8,0},{12,4},{1,9},{5,13},{9,1},{13,5},{2,10},{6,14},... | collective-permute-start | bytes 147464 | tf_op jit(solution)/shard_map/ppermute | solution.py:115
  38.3 3.9 %collective-permute-start.10 = (f32[48,128]{1,0:T(8,128)S(1)}, f32[48,128]{1,0:T(8,128)S(1)}, u32[]{:S(2)}, u32[]{:S(2)}) collective-permute-start(f32[48,128]{1,0:T(8,128)S(1)} %slice.29), channel_id=1, source_target_pairs={{0,2},{1,3},{2,0},{3,1},{4,6},{5,7},{6,4},{7,5},{8,10},{9,11},{10,... | collective-permute-start | bytes 73736 | tf_op jit(solution)/shard_map/ppermute | solution.py:123

commit v4 on v3

--- a/solution.py
+++ b/solution.py
@@ -25,11 +25,30 @@
     return parts * np.float32(1.0 / math.sqrt(freqs))
 
 
+def halves(table):
+    hi = table.astype(ml_dtypes.bfloat16)
+    return hi, (table - hi.astype(np.float32)).astype(ml_dtypes.bfloat16)
+
+
+def turned(lags):
+    return np.concatenate([[0], np.arange(lags // 2 - 1, 0, -1)])
+
+
 def split_table(freqs, lags):
     table = dft_table(freqs, lags)
-    hi = table.astype(ml_dtypes.bfloat16)
-    lo = (table - hi.astype(np.float32)).astype(ml_dtypes.bfloat16)
-    return [jnp.asarray(t) for t in (hi, lo, hi.T.copy(), lo.T.copy())]
+    mid = lags // 2
+    th, tl = halves(table[:, np.concatenate([np.arange(mid, lags), turned(lags)])])
+    even, odd = table[:freqs, mid:].T, table[freqs:, mid:].T.copy()
+    odd[0] = table[freqs:, 0]
+    ch, cl = halves(even)
+    sh, sl = halves(odd)
+    eh, el = halves(table[:freqs, 0])
+    rest = np.zeros((mid, freqs), ml_dtypes.bfloat16)
+    rest[0], rest[1], rest[2] = eh, eh, el
+    back = [np.concatenate([ch, ch, cl, rest], 0), np.concatenate([sh, sh, sl], 0)]
+    move = np.zeros((mid, mid), ml_dtypes.bfloat16)
+    move[turned(lags), np.arange(mid)] = 1
+    return [jnp.asarray(t) for t in (th, tl, *back, np.concatenate([move] * 3, 0))]
 
 
 def split(x):
@@ -68,6 +87,32 @@
         ),
     )(*arrays)
     return kept[: len(vectors)], kept[len(vectors) :]
+
+
+def turn_kernel(seen, move, after, out):
+    rows, pairs_in, lags = seen.shape
+    mid = lags // 2
+    out[:, :, :mid] = seen[:, :, mid:]
+    count = 8
+    for p in range(0, rows, count):
+        low = seen[p : p + count, :, :mid].reshape(count * pairs_in, mid)
+        high, rest = low.astype(bf16), low - low.astype(bf16).astype(f32)
+        parts = jnp.concatenate([high, *split(rest)], 1)
+        out[p : p + count, :, mid:] = dot(parts, move[...]).reshape(count, pairs_in, mid)
+
+
+def turn(seen, move, after):
+    vmem = pl.BlockSpec(memory_space=pltpu.VMEM)
+    return pl.pallas_call(
+        turn_kernel,
+        in_specs=[vmem, vmem, pl.BlockSpec(memory_space=pl.ANY)],
+        out_specs=vmem,
+        out_shape=pltpu.VMEM(seen.shape, seen.dtype),
+        compiler_params=pltpu.CompilerParams(vmem_limit_bytes=32 * 2**20),
+        cost_estimate=pl.CostEstimate(
+            flops=3 * seen.size * seen.shape[2], bytes_accessed=8 * seen.size, transcendentals=0
+        ),
+    )(seen, move, after)
 
 
 def bits_of(n):
@@ -169,11 +214,26 @@
     return dot(jnp.concatenate(left, 1), jnp.concatenate(right, 0))
 
 
-def spectral_part(c, chunks, wh, wl, bh, bl):
-    size = bh.shape[1] // chunks
-    at = slice(c * size, (c + 1) * size)
-    left = jnp.concatenate([wh, wl, wh], 1)
-    return at, dot(left, jnp.concatenate([bh[:, at], bh[:, at], bl[:, at]], 0))
+def fold(weighted, mid):
+    up, down = weighted[:, :mid], weighted[:, mid:]
+    column = lax.broadcasted_iota(jnp.int32, up.shape, 1)
+    even = jnp.where(column == 0, up, up + down)
+    odd = jnp.where(column == 0, down, up - down)
+    lone = jnp.broadcast_to(down[:, :1], down.shape)
+    high = lone.astype(bf16).astype(f32)
+    lone = jnp.where(column == 1, lone - high, high).astype(bf16)
+    return (*split(even), lone, *split(odd))
+
+
+def spectral_part(c, chunks, folded, span, bc, bs, mid):
+    size = 2 * LANES
+    eh, el, lone, oh, ol = [folded[span, k * mid : (k + 1) * mid] for k in range(5)]
+    if c < chunks // 2:
+        left, right, here = [eh, el, eh, lone], bc, c
+    else:
+        left, right, here = [oh, ol, oh], bs, c - chunks // 2
+    value = dot(jnp.concatenate(left, 1), right[:, here * size : (here + 1) * size])
+    return slice(c * size, (c + 1) * size), value
 
 
 def adjoint_rows(chunks, p0, count, spec, ua, ub, rows, cols, tile, half):
@@ -225,7 +285,7 @@
 ):
     held, refs = refs[:n_held], refs[n_held:]
     tile, half = None, None
-    (th, tl, bh, bl), refs = refs[:4], refs[4:]
+    (th, tl, bc, bs), refs = refs[:4], refs[4:]
     per = geometry[3]
     half = th.shape[0] // 2
     lags = th.shape[1]
@@ -240,7 +300,7 @@
     xh, xl, spec = refs[5:7], refs[7:9], refs[9:11]
     tile = ua.shape[0]
     if backward:
-        wh, wl = refs[11:]
+        (folded,) = refs[11:]
     place_stations(held, place, me, blocked, geometry)
     load_block(blocked, tiles[0, 0], ua, tile, per)
     load_block(blocked, tiles[0, 1], ub, tile, per)
@@ -259,14 +319,14 @@
         if backward:
             misfit = lagged - seen[i * step : (i + 1) * step].reshape(step * tile, lags)
             weighted = misfit + cubic_weight * misfit * misfit * misfit
-            wh[span, :], wl[span, :] = split(weighted)
+            folded[span, :] = jnp.concatenate(fold(weighted, lags // 2), 1)
         else:
             lagged_out[span, :] = lagged
 
     def spectral_step(i, c):
         if i < steps:
             span = slice(i * step * tile, (i + 1) * step * tile)
-            at, value = spectral_part(c, chunks, wh[span, :], wl[span, :], bh, bl)
+            at, value = spectral_part(c, chunks, folded, span, bc, bs, lags // 2)
             spec[i % 2][:, at] = value
 
     cross_step(0, range(chunks))
@@ -319,8 +379,7 @@
             specs.append(vmem)
         out_shape = [jax.ShapeDtypeStruct((count * per // n_out, LANES), f32)] * n_out
         scratch += [
-            pltpu.VMEM((tile * tile, lags), bf16),
-            pltpu.VMEM((tile * tile, lags), bf16),
+            pltpu.VMEM((tile * tile, 5 * (lags // 2)), bf16),
         ]
     else:
         out_shape = [jax.ShapeDtypeStruct((tile * tile, lags), f32)]
@@ -349,6 +408,8 @@
     tables = split_table(width // 2, observed.shape[3])
     (own, seen, *tables), (tiles, place, me) = stage([piece, observed[0], *tables], [tiles, place, me])
     held = gather(piece, own, sta, band)
+    *tables, move = tables
+    seen = turn(seen, move, held[0])
     if src == 1:
         parts = tile_call(geometry, tiles, place, me, held, tables, seen)
     else:

time: 42.9 us -> 42 us (0.979)
  waiting for transfers between devices: 14.5 us -> 13.7 us
    pallas_call x1, Pallas kernels: 12.1 us -> 11.2 us  [tile_call(): pl.pallas_call(functools.partial(tile_kernel, geometry, len(held), n_out,...]
    ppermute x3, waiting for transfers between devices: 4.42 us -> 3.65 us  [gather(): held = held + [lax.ppermute(one, 'band', pairs(band, bit)) for one in held]]
    pallas_call x0 -> x1, Pallas kernels: none -> 0.76 us  [turn(): pl.pallas_call(turn_kernel, in_specs=[vmem, vmem, pl.BlockSpec(memory_spa...]
  transfers between devices with their start and end apart: 11 -> 11, of which waited for: 9 -> 9; matrix products, arithmetic and copies ran while one was open for 1% -> 1% of each run, Pallas kernels for 5% -> 7%
where the time goes in v4:
time: 42 us; the launch traced here: 41.9 us
  Pallas kernels  14.2 us (34%)
  waiting for transfers between devices  13.7 us (33%)
  starting transfers between devices  12.5 us (30%)
  other arithmetic  1.27 us (3%)
    pallas_call x1, Pallas kernels, tile_call(): pl.pallas_call(functools.partial(tile_kernel, geometry, len(held), n_out,...  11.2 us
    ppermute x3, starting transfers between devices, gather(): lax.ppermute(piece, 'sta', pairs(sta, k))  5.62 us
    ppermute x3, waiting for transfers between devices, scatter_sum(): lax.ppermute(total[k * each:(k + 1) * each], 'sta', pairs(sta, k))  5.03 us
    ppermute x3, waiting for transfers between devices, gather(): held = held + [lax.ppermute(one, 'band', pairs(band, bit)) for one in held]  3.65 us
    ppermute x3, starting transfers between devices, scatter_sum(): lax.ppermute(total[k * each:(k + 1) * each], 'sta', pairs(sta, k))  3.58 us
    ppermute x1, waiting for transfers between devices, scatter_sum(): total = total[:half] + lax.ppermute(total[half:], 'band', pairs(band, bit))  2.34 us
    pallas_call x1, Pallas kernels, stage(): pl.pallas_call(stage_kernel, in_specs=[pl.BlockSpec(memory_space=pl.ANY)]...  2.32 us
    ppermute x3, starting transfers between devices, gather(): held = held + [lax.ppermute(one, 'band', pairs(band, bit)) for one in held]  1.56 us
  transfers between devices with their start and end apart: 11, of which 9 were waited for; matrix products, arithmetic and copies ran while one was open for 1% of the time, Pallas kernels for 7%

profile of v4, /device:TPU:0, one launch (start us, length us, event | category | flops | bytes accessed | tf_op | source)
XLA Modules:
  0.0 41.9 jit_solution(8034704835577301953)
XLA Ops:
  0.0 5.0 %collective-permute-start.2 = (f32[48,128]{1,0:T(8,128)}, f32[48,128]{1,0:T(8,128)S(1)}, u32[]{:S(2)}, u32[]{:S(2)}) collective-permute-start(f32[48,128]{1,0:T(8,128)} %bitcast.6), channel_id=1, source_target_pairs={{0,12},{4,8},{8,4},{12,0},{1,13},{5,9},{9,5},{13,1},{2,14},{6,10},... | collective-permute-start | bytes 73736 | tf_op jit(solution)/shard_map/ppermute | solution.py:145
  5.0 0.0 collective-permute-start.1
  5.1 0.6 %collective-permute-start = (f32[48,128]{1,0:T(8,128)}, f32[48,128]{1,0:T(8,128)S(1)}, u32[]{:S(2)}, u32[]{:S(2)}) collective-permute-start(f32[48,128]{1,0:T(8,128)} %bitcast.8), channel_id=1, source_target_pairs={{0,4},{4,0},{8,12},{12,8},{1,5},{5,1},{9,13},{13,9},{2,6},{6,2},{1... | collective-permute-start | bytes 73736 | tf_op jit(solution)/shard_map/ppermute | solution.py:145
  5.6 0.6 %pad_add_fusion.refs_9_ = s32[2]{0:T(128)} fusion(s32[1]{0:T(128)} %bitcast.3, s32[1]{0:T(128)} %bitcast.2), kind=kLoop, calls=%fused_computation.8 | loop fusion | flops 2 | bytes 16 | tf_op jit(solution)/shard_map/stack | solution.py:407
  6.2 2.3 %shard_map.91 = (f32[48,128]{1,0:T(8,128)S(1)}, f32[48,48,256]{2,1,0:T(8,128)S(1)}, bf16[1024,256]{1,0:T(8,128)(2,1)S(1)}, bf16[1024,256]{1,0:T(8,128)(2,1)S(1)}...) custom-call(f32[48,128]{1,0:T(8,128)} %bitcast.9, ...), custom_call_target="tpu_custom_call" | custom-call | bytes 8896512 | tf_op jit(solution)/shard_map/pallas_call | solution.py:77
  8.6 0.5 %collective-permute-done = f32[48,128]{1,0:T(8,128)S(1)} collective-permute-done((f32[48,128]{1,0:T(8,128)}, f32[48,128]{1,0:T(8,128)S(1)}, u32[]{:S(2)}, u32[]{:S(2)}) %collective-permute-start) | collective-permute-done | bytes 24608 | tf_op jit(solution)/shard_map/ppermute | solution.py:145
  9.1 0.9 %collective-permute-done.1 = f32[48,128]{1,0:T(8,128)S(1)} collective-permute-done((f32[48,128]{1,0:T(8,128)}, f32[48,128]{1,0:T(8,128)S(1)}, u32[]{:S(2)}, u32[]{:S(2)}) %collective-permute-start.1) | collective-permute-done | bytes 24608 | tf_op jit(solution)/shard_map/ppermute | solution.py:145
  10.0 0.0 collective-permute-done.2
  10.0 1.6 %collective-permute-start.3 = (f32[192,128]{1,0:T(8,128)S(1)}, f32[192,128]{1,0:T(8,128)S(1)}, u32[]{:S(2)}, u32[]{:S(2)}) collective-permute-start(f32[192,128]{1,0:T(8,128)S(1)} %constant_dynamic-update-slice_fusion.after.refs_0_), channel_id=1, source_target_pairs={{0,2},{1,3},{2,0},{3,1},{4,6},{5,7},{6,4},{7,5},{8,10},{9,11},{10,... | collective-permute-start | bytes 294920 | tf_op jit(solution)/shard_map/ppermute | solution.py:148
  11.6 0.0 collective-permute-start.4
  11.6 3.1 %collective-permute-done.3.refs_1_ = f32[192,128]{1,0:T(8,128)S(1)} collective-permute-done((f32[192,128]{1,0:T(8,128)S(1)}, f32[192,128]{1,0:T(8,128)S(1)}, u32[]{:S(2)}, u32[]{:S(2)}) %collective-permute-start.3) | collective-permute-done | bytes 98336 | tf_op jit(solution)/shard_map/ppermute | solution.py:148
  14.7 0.0 collective-permute-start.5
  14.7 0.8 %shard_map.92.refs_8_ = f32[48,48,256]{2,1,0:T(8,128)S(1)} custom-call(f32[48,48,256]{2,1,0:T(8,128)S(1)} %get-tuple-element.25.seen, bf16[384,128]{1,0:T(8,128)(2,1)S(1)} %get-tuple-element.26.move, f32[192,128]{1,0:T(8,128)S(1)} %constant_dynamic-update-slice_fusion.after.refs_0_), custom_call_target="tpu_custom_call" | custom-call | flops 452984832 | bytes 4718592 | tf_op jit(solution)/shard_map/pallas_call | solution.py:106
  15.5 0.0 collective-permute-done.4.refs_2_
  15.5 0.5 %collective-permute-done.5.refs_3_ = f32[192,128]{1,0:T(8,128)S(1)} collective-permute-done((f32[192,128]{1,0:T(8,128)S(1)}, f32[192,128]{1,0:T(8,128)S(1)}, u32[]{:S(2)}, u32[]{:S(2)}) %collective-permute-start.5) | collective-permute-done | bytes 98336 | tf_op jit(solution)/shard_map/ppermute | solution.py:148
  16.0 11.2 %shard_map.93 = (f32[384,128]{1,0:T(8,128)S(1)}, f32[384,128]{1,0:T(8,128)S(1)}) custom-call(s32[1,2]{1,0:T(1,128)S(4)} %get-tuple-element.17.tiles, s32[96]{0:T(128)S(4)} %get-tuple-element.18.place, s32[2]{0:T(128)S(4)} %get-tuple-element.19.me, f32[192,128]{1,0:T(8,128)S(1)} %constant_dynamic-update-slice_fusion.after.refs_0_, ...), custom_call_target="tpu_custom_call" | custom-call | flops 7247757312 | bytes 9437184 | tf_op jit(solution)/shard_map/pallas_call | solution.py:387
  27.2 0.2 collective-permute-start.6
  27.4 1.3 %collective-permute-done.6 = f32[384,128]{1,0:T(8,128)S(1)} collective-permute-done((f32[384,128]{1,0:T(8,128)S(1)}, f32[384,128]{1,0:T(8,128)S(1)}, u32[]{:S(2)}, u32[]{:S(2)}) %collective-permute-start.6) | collective-permute-done | bytes 196640 | tf_op jit(solution)/shard_map/ppermute | solution.py:156
  28.7 0.2 collective-permute-start.7
  28.9 3.4 %collective-permute-start.9 = (f32[96,128]{1,0:T(8,128)S(1)}, f32[96,128]{1,0:T(8,128)S(1)}, u32[]{:S(2)}, u32[]{:S(2)}) collective-permute-start(f32[96,128]{1,0:T(8,128)S(1)} %get-tuple-element.30), channel_id=1, source_target_pairs={{0,12},{4,8},{8,4},{12,0},{1,13},{5,9},{9,5},{13,1},{2,14},{6,10},... | collective-permute-start | bytes 147464 | tf_op jit(solution)/shard_map/ppermute | solution.py:160
  32.3 0.0 collective-permute-start.8
  32.3 0.6 %collective-permute-done.7 = f32[96,128]{1,0:T(8,128)S(1)} collective-permute-done((f32[96,128]{1,0:T(8,128)S(1)}, f32[96,128]{1,0:T(8,128)S(1)}, u32[]{:S(2)}, u32[]{:S(2)}) %collective-permute-start.7) | collective-permute-done | bytes 49184 | tf_op jit(solution)/shard_map/ppermute | solution.py:160
  32.9 2.5 %collective-permute-done.9 = f32[96,128]{1,0:T(8,128)S(1)} collective-permute-done((f32[96,128]{1,0:T(8,128)S(1)}, f32[96,128]{1,0:T(8,128)S(1)}, u32[]{:S(2)}, u32[]{:S(2)}) %collective-permute-start.9) | collective-permute-done | bytes 49184 | tf_op jit(solution)/shard_map/ppermute | solution.py:160
  35.3 2.0 %collective-permute-done.8 = f32[96,128]{1,0:T(8,128)S(1)} collective-permute-done((f32[96,128]{1,0:T(8,128)S(1)}, f32[96,128]{1,0:T(8,128)S(1)}, u32[]{:S(2)}, u32[]{:S(2)}) %collective-permute-start.8) | collective-permute-done | bytes 49184 | tf_op jit(solution)/shard_map/ppermute | solution.py:160
  37.4 1.6 %collective-permute-start.10 = (f32[48,128]{1,0:T(8,128)S(1)}, f32[48,128]{1,0:T(8,128)S(1)}, u32[]{:S(2)}, u32[]{:S(2)}) collective-permute-start(f32[48,128]{1,0:T(8,128)S(1)} %slice.29), channel_id=1, source_target_pairs={{0,2},{1,3},{2,0},{3,1},{4,6},{5,7},{6,4},{7,5},{8,10},{9,11},{10,... | collective-permute-start | bytes 73736 | tf_op jit(solution)/shard_map/ppermute | solution.py:168
  38.9 2.3 %collective-permute-done.10 = f32[48,128]{1,0:T(8,128)S(1)} collective-permute-done((f32[48,128]{1,0:T(8,128)S(1)}, f32[48,128]{1,0:T(8,128)S(1)}, u32[]{:S(2)}, u32[]{:S(2)}) %collective-permute-start.10) | collective-permute-done | bytes 24608 | tf_op jit(solution)/shard_map/ppermute | solution.py:168
  41.3 0.6 %slice_add_fusion.1 = f32[48,128]{1,0:T(8,128)} fusion(f32[48,128]{1,0:T(8,128)S(1)} %collective-permute-done.10, f32[96,128]{1,0:T(8,128)S(1)} %fusion.1), kind=kLoop, calls=%fused_computation.3 | loop fusion | flops 6144 | bytes 73728 | tf_op jit(solution)/shard_map/add | solution.py:168
  (8 shorter events, 0.1 us)
Async XLA Ops:
  0.0 10.0 %collective-permute-start.2 = (f32[48,128]{1,0:T(8,128)}, f32[48,128]{1,0:T(8,128)S(1)}, u32[]{:S(2)}, u32[]{:S(2)}) collective-permute-start(f32[48,128]{1,0:T(8,128)} %bitcast.6), channel_id=1, source_target_pairs={{0,12},{4,8},{8,4},{12,0},{1,13},{5,9},{9,5},{13,1},{2,14},{6,10},... | collective-permute-start | bytes 73736 | tf_op jit(solution)/shard_map/ppermute | solution.py:145
  5.0 4.9 %collective-permute-start.1 = (f32[48,128]{1,0:T(8,128)}, f32[48,128]{1,0:T(8,128)S(1)}, u32[]{:S(2)}, u32[]{:S(2)}) collective-permute-start(f32[48,128]{1,0:T(8,128)} %bitcast.7), channel_id=1, source_target_pairs={{0,8},{4,12},{8,0},{12,4},{1,9},{5,13},{9,1},{13,5},{2,10},{6,14},... | collective-permute-start | bytes 73736 | tf_op jit(solution)/shard_map/ppermute | solution.py:145
  5.1 4.0 %collective-permute-start = (f32[48,128]{1,0:T(8,128)}, f32[48,128]{1,0:T(8,128)S(1)}, u32[]{:S(2)}, u32[]{:S(2)}) collective-permute-start(f32[48,128]{1,0:T(8,128)} %bitcast.8), channel_id=1, source_target_pairs={{0,4},{4,0},{8,12},{12,8},{1,5},{5,1},{9,13},{13,9},{2,6},{6,2},{1... | collective-permute-start | bytes 73736 | tf_op jit(solution)/shard_map/ppermute | solution.py:145
  10.0 4.7 %collective-permute-start.3 = (f32[192,128]{1,0:T(8,128)S(1)}, f32[192,128]{1,0:T(8,128)S(1)}, u32[]{:S(2)}, u32[]{:S(2)}) collective-permute-start(f32[192,128]{1,0:T(8,128)S(1)} %constant_dynamic-update-slice_fusion.after.refs_0_), channel_id=1, source_target_pairs={{0,2},{1,3},{2,0},{3,1},{4,6},{5,7},{6,4},{7,5},{8,10},{9,11},{10,... | collective-permute-start | bytes 294920 | tf_op jit(solution)/shard_map/ppermute | solution.py:148
  11.6 3.9 %collective-permute-start.4 = (f32[192,128]{1,0:T(8,128)S(1)}, f32[192,128]{1,0:T(8,128)S(1)}, u32[]{:S(2)}, u32[]{:S(2)}) collective-permute-start(f32[192,128]{1,0:T(8,128)S(1)} %constant_dynamic-update-slice_fusion.after.refs_0_), channel_id=1, source_target_pairs={{0,1},{1,0},{2,3},{3,2},{4,5},{5,4},{6,7},{7,6},{8,9},{9,8},{10,11... | collective-permute-start | bytes 294920 | tf_op jit(solution)/shard_map/ppermute | solution.py:148
  14.7 1.3 %collective-permute-start.5 = (f32[192,128]{1,0:T(8,128)S(1)}, f32[192,128]{1,0:T(8,128)S(1)}, u32[]{:S(2)}, u32[]{:S(2)}) collective-permute-start(f32[192,128]{1,0:T(8,128)S(1)} %collective-permute-done.3.refs_1_), channel_id=1, source_target_pairs={{0,1},{1,0},{2,3},{3,2},{4,5},{5,4},{6,7},{7,6},{8,9},{9,8},{10,11... | collective-permute-start | bytes 294920 | tf_op jit(solution)/shard_map/ppermute | solution.py:148
  27.2 1.5 %collective-permute-start.6 = (f32[384,128]{1,0:T(8,128)S(1)}, f32[384,128]{1,0:T(8,128)S(1)}, u32[]{:S(2)}, u32[]{:S(2)}) collective-permute-start(f32[384,128]{1,0:T(8,128)S(1)} %get-tuple-element.28), channel_id=1, source_target_pairs={{0,1},{1,0},{2,3},{3,2},{4,5},{5,4},{6,7},{7,6},{8,9},{9,8},{10,11... | collective-permute-start | bytes 589832 | tf_op jit(solution)/shard_map/ppermute | solution.py:156
  28.7 4.2 %collective-permute-start.7 = (f32[96,128]{1,0:T(8,128)S(1)}, f32[96,128]{1,0:T(8,128)S(1)}, u32[]{:S(2)}, u32[]{:S(2)}) collective-permute-start(f32[96,128]{1,0:T(8,128)S(1)} %get-tuple-element.29), channel_id=1, source_target_pairs={{0,4},{4,0},{8,12},{12,8},{1,5},{5,1},{9,13},{13,9},{2,6},{6,2},{1... | collective-permute-start | bytes 147464 | tf_op jit(solution)/shard_map/ppermute | solution.py:160
  28.9 6.5 %collective-permute-start.9 = (f32[96,128]{1,0:T(8,128)S(1)}, f32[96,128]{1,0:T(8,128)S(1)}, u32[]{:S(2)}, u32[]{:S(2)}) collective-permute-start(f32[96,128]{1,0:T(8,128)S(1)} %get-tuple-element.30), channel_id=1, source_target_pairs={{0,12},{4,8},{8,4},{12,0},{1,13},{5,9},{9,5},{13,1},{2,14},{6,10},... | collective-permute-start | bytes 147464 | tf_op jit(solution)/shard_map/ppermute | solution.py:160
  32.3 5.0 %collective-permute-start.8 = (f32[96,128]{1,0:T(8,128)S(1)}, f32[96,128]{1,0:T(8,128)S(1)}, u32[]{:S(2)}, u32[]{:S(2)}) collective-permute-start(f32[96,128]{1,0:T(8,128)S(1)} %get-tuple-element.31), channel_id=1, source_target_pairs={{0,8},{4,12},{8,0},{12,4},{1,9},{5,13},{9,1},{13,5},{2,10},{6,14},... | collective-permute-start | bytes 147464 | tf_op jit(solution)/shard_map/ppermute | solution.py:160
  37.4 3.9 %collective-permute-start.10 = (f32[48,128]{1,0:T(8,128)S(1)}, f32[48,128]{1,0:T(8,128)S(1)}, u32[]{:S(2)}, u32[]{:S(2)}) collective-permute-start(f32[48,128]{1,0:T(8,128)S(1)} %slice.29), channel_id=1, source_target_pairs={{0,2},{1,3},{2,0},{3,1},{4,6},{5,7},{6,4},{7,5},{8,10},{9,11},{10,... | collective-permute-start | bytes 73736 | tf_op jit(solution)/shard_map/ppermute | solution.py:168

commit v5 on v4

--- a/solution.py
+++ b/solution.py
@@ -173,10 +173,10 @@
     return ((offset[0] ^ me[0]) * band + (offset[1] ^ me[1])) * rows
 
 
-def place_stations(held, place, me, blocked, geometry):
+def place_stations(held, place, blocked, geometry):
     sta, band, rows, per = geometry
     order = gather_order(sta, band)
-    here = (me[0], me[1])
+    here = (lax.axis_index("sta"), lax.axis_index("band"))
     at = 0
     for ref in held:
         for n in range(ref.shape[0] // (rows * per)):
@@ -258,7 +258,7 @@
         rows[p0 : p0 + count, im] = jnp.concatenate(rim, 0)
 
 
-def give_terms(tiles, place, me, rows, cols, blocked, outs, geometry, tile):
+def give_terms(tiles, place, rows, cols, blocked, outs, geometry, tile):
     sta, band, nrows, per = geometry
     scale = 1.0 / tile
     blocked[...] = jnp.zeros_like(blocked)
@@ -268,7 +268,7 @@
             spot = pl.ds(j, tile, stride=per)
             view[spot, :] = view[spot, :] + ref[:, j * LANES : (j + 1) * LANES]
     order = scatter_order(sta, band)
-    here = (me[0], me[1])
+    here = (lax.axis_index("sta"), lax.axis_index("band"))
     at = 0
     for out in outs:
         for n in range(out.shape[0] // (nrows * per)):
@@ -281,7 +281,7 @@
 
 
 def tile_kernel(
-    geometry, n_held, n_out, step, forward, backward, tiles, place, me, *refs
+    geometry, n_held, n_out, step, forward, backward, tiles, place, *refs
 ):
     held, refs = refs[:n_held], refs[n_held:]
     tile, half = None, None
@@ -301,7 +301,7 @@
     tile = ua.shape[0]
     if backward:
         (folded,) = refs[11:]
-    place_stations(held, place, me, blocked, geometry)
+    place_stations(held, place, blocked, geometry)
     load_block(blocked, tiles[0, 0], ua, tile, per)
     load_block(blocked, tiles[0, 1], ub, tile, per)
     if backward:
@@ -348,19 +348,19 @@
                 spectral_step(i + 1, c)
                 adjoint_rows([c], i * step, step, spec[i % 2], ua, ub, rows, cols, tile, half)
     if backward:
-        give_terms(tiles, place, me, rows, cols, blocked, outs, geometry, tile)
-
-
-def tile_call(geometry, tiles, place, me, held, tables, seen, lagged=None, forward=True, backward=True):
+        give_terms(tiles, place, rows, cols, blocked, outs, geometry, tile)
+
+
+def tile_call(geometry, tiles, place, held, tables, seen, lagged=None, forward=True, backward=True):
     sta, band, rows, per = geometry
     tile, lags = seen.shape[1:]
     width = per * LANES
-    step = 16
+    step = 24
     count = place.shape[0]
     smem = pl.BlockSpec(memory_space=pltpu.SMEM)
     vmem = pl.BlockSpec(memory_space=pltpu.VMEM)
-    args = [tiles, place, me, *held, *tables]
-    specs = [smem] * 3 + [vmem] * (len(held) + 4)
+    args = [tiles, place, *held, *tables]
+    specs = [smem] * 2 + [vmem] * (len(held) + 4)
     n_out = 2 if band > 1 else 1
     scratch = [
         pltpu.VMEM((count * per, LANES), f32),
@@ -404,18 +404,17 @@
     per = width // LANES
     geometry = (sta, band, rows, per)
     piece = spectra.reshape(rows * per, LANES)
-    me = jnp.stack([lax.axis_index("sta"), lax.axis_index("band")]).astype(jnp.int32)
     tables = split_table(width // 2, observed.shape[3])
-    (own, seen, *tables), (tiles, place, me) = stage([piece, observed[0], *tables], [tiles, place, me])
+    (own, seen, *tables), (tiles, place) = stage([piece, observed[0], *tables], [tiles, place])
     held = gather(piece, own, sta, band)
     *tables, move = tables
     seen = turn(seen, move, held[0])
     if src == 1:
-        parts = tile_call(geometry, tiles, place, me, held, tables, seen)
+        parts = tile_call(geometry, tiles, place, held, tables, seen)
     else:
-        (lagged,) = tile_call(geometry, tiles, place, me, held, tables, seen, backward=False)
+        (lagged,) = tile_call(geometry, tiles, place, held, tables, seen, backward=False)
         lagged = lax.psum(lagged, "src")
-        parts = tile_call(geometry, tiles, place, me, held, tables, seen, lagged, forward=False)
+        parts = tile_call(geometry, tiles, place, held, tables, seen, lagged, forward=False)
     return scatter_sum(parts, sta, band).reshape(spectra.shape)
 
 

time: 42 us -> 41.7 us (level)
  other arithmetic: 1.27 us -> 0.65 us
  waiting for transfers between devices: 13.7 us -> 14.3 us
    ppermute x3, waiting for transfers between devices: 1.41 us -> 2.04 us  [gather(): lax.ppermute(piece, 'sta', pairs(sta, k))]
    another operation x1 -> x0, other arithmetic: 0.62 us -> none  [local(): jnp.stack([lax.axis_index('sta'), lax.axis_index('band')]).astype(jnp.int32)]
  transfers between devices with their start and end apart: 11 -> 11, of which waited for: 9 -> 9; matrix products, arithmetic and copies ran while one was open for 1% -> 0% of each run, Pallas kernels for 7% -> 7%
where the time goes in v5:
time: 41.7 us; the launch traced here: 41.5 us
  waiting for transfers between devices  14.3 us (34%)
  Pallas kernels  13.9 us (33%)
  starting transfers between devices  12.5 us (30%)
  other arithmetic  0.65 us (2%)
    pallas_call x1, Pallas kernels, tile_call(): pl.pallas_call(functools.partial(tile_kernel, geometry, len(held), n_out,...  10.9 us
    ppermute x3, starting transfers between devices, gather(): lax.ppermute(piece, 'sta', pairs(sta, k))  5.62 us
    ppermute x3, waiting for transfers between devices, scatter_sum(): lax.ppermute(total[k * each:(k + 1) * each], 'sta', pairs(sta, k))  4.98 us
    ppermute x3, waiting for transfers between devices, gather(): held = held + [lax.ppermute(one, 'band', pairs(band, bit)) for one in held]  3.65 us
    ppermute x3, starting transfers between devices, scatter_sum(): lax.ppermute(total[k * each:(k + 1) * each], 'sta', pairs(sta, k))  3.58 us
    ppermute x1, waiting for transfers between devices, scatter_sum(): total = total[:half] + lax.ppermute(total[half:], 'band', pairs(band, bit))  2.34 us
    pallas_call x1, Pallas kernels, stage(): pl.pallas_call(stage_kernel, in_specs=[pl.BlockSpec(memory_space=pl.ANY)]...  2.31 us
    ppermute x3, waiting for transfers between devices, gather(): lax.ppermute(piece, 'sta', pairs(sta, k))  2.04 us
  transfers between devices with their start and end apart: 11, of which 9 were waited for; matrix products, arithmetic and copies ran while one was open for 0% of the time, Pallas kernels for 7%

profile of v5, /device:TPU:0, one launch (start us, length us, event | category | flops | bytes accessed | tf_op | source)
XLA Modules:
  0.0 41.5 jit_solution(13814437249688473320)
XLA Ops:
  0.0 5.0 %collective-permute-start.2 = (f32[48,128]{1,0:T(8,128)}, f32[48,128]{1,0:T(8,128)S(1)}, u32[]{:S(2)}, u32[]{:S(2)}) collective-permute-start(f32[48,128]{1,0:T(8,128)} %bitcast.4), channel_id=1, source_target_pairs={{0,12},{4,8},{8,4},{12,0},{1,13},{5,9},{9,5},{13,1},{2,14},{6,10},... | collective-permute-start | bytes 73736 | tf_op jit(solution)/shard_map/ppermute | solution.py:145
  5.0 0.0 collective-permute-start.1
  5.1 0.6 %collective-permute-start = (f32[48,128]{1,0:T(8,128)}, f32[48,128]{1,0:T(8,128)S(1)}, u32[]{:S(2)}, u32[]{:S(2)}) collective-permute-start(f32[48,128]{1,0:T(8,128)} %bitcast.6), channel_id=1, source_target_pairs={{0,4},{4,0},{8,12},{12,8},{1,5},{5,1},{9,13},{13,9},{2,6},{6,2},{1... | collective-permute-start | bytes 73736 | tf_op jit(solution)/shard_map/ppermute | solution.py:145
  5.6 2.3 %shard_map.91 = (f32[48,128]{1,0:T(8,128)S(1)}, f32[48,48,256]{2,1,0:T(8,128)S(1)}, bf16[1024,256]{1,0:T(8,128)(2,1)S(1)}, bf16[1024,256]{1,0:T(8,128)(2,1)S(1)}...) custom-call(f32[48,128]{1,0:T(8,128)} %bitcast.7, ...), custom_call_target="tpu_custom_call" | custom-call | bytes 8896512 | tf_op jit(solution)/shard_map/pallas_call | solution.py:77
  7.9 1.1 %collective-permute-done = f32[48,128]{1,0:T(8,128)S(1)} collective-permute-done((f32[48,128]{1,0:T(8,128)}, f32[48,128]{1,0:T(8,128)S(1)}, u32[]{:S(2)}, u32[]{:S(2)}) %collective-permute-start) | collective-permute-done | bytes 24608 | tf_op jit(solution)/shard_map/ppermute | solution.py:145
  9.1 0.9 %collective-permute-done.1 = f32[48,128]{1,0:T(8,128)S(1)} collective-permute-done((f32[48,128]{1,0:T(8,128)}, f32[48,128]{1,0:T(8,128)S(1)}, u32[]{:S(2)}, u32[]{:S(2)}) %collective-permute-start.1) | collective-permute-done | bytes 24608 | tf_op jit(solution)/shard_map/ppermute | solution.py:145
  10.0 0.0 collective-permute-done.2
  10.0 1.6 %collective-permute-start.3 = (f32[192,128]{1,0:T(8,128)S(1)}, f32[192,128]{1,0:T(8,128)S(1)}, u32[]{:S(2)}, u32[]{:S(2)}) collective-permute-start(f32[192,128]{1,0:T(8,128)S(1)} %constant_dynamic-update-slice_fusion.after.refs_0_), channel_id=1, source_target_pairs={{0,2},{1,3},{2,0},{3,1},{4,6},{5,7},{6,4},{7,5},{8,10},{9,11},{10,... | collective-permute-start | bytes 294920 | tf_op jit(solution)/shard_map/ppermute | solution.py:148
  11.6 0.0 collective-permute-start.4
  11.6 3.1 %collective-permute-done.3.refs_1_ = f32[192,128]{1,0:T(8,128)S(1)} collective-permute-done((f32[192,128]{1,0:T(8,128)S(1)}, f32[192,128]{1,0:T(8,128)S(1)}, u32[]{:S(2)}, u32[]{:S(2)}) %collective-permute-start.3) | collective-permute-done | bytes 98336 | tf_op jit(solution)/shard_map/ppermute | solution.py:148
  14.7 0.0 collective-permute-start.5
  14.7 0.8 %shard_map.92.refs_8_ = f32[48,48,256]{2,1,0:T(8,128)S(1)} custom-call(f32[48,48,256]{2,1,0:T(8,128)S(1)} %get-tuple-element.23.seen, bf16[384,128]{1,0:T(8,128)(2,1)S(1)} %get-tuple-element.24.move, f32[192,128]{1,0:T(8,128)S(1)} %constant_dynamic-update-slice_fusion.after.refs_0_), custom_call_target="tpu_custom_call" | custom-call | flops 452984832 | bytes 4718592 | tf_op jit(solution)/shard_map/pallas_call | solution.py:106
  15.5 0.0 collective-permute-done.4.refs_2_
  15.5 0.5 %collective-permute-done.5.refs_3_ = f32[192,128]{1,0:T(8,128)S(1)} collective-permute-done((f32[192,128]{1,0:T(8,128)S(1)}, f32[192,128]{1,0:T(8,128)S(1)}, u32[]{:S(2)}, u32[]{:S(2)}) %collective-permute-start.5) | collective-permute-done | bytes 98336 | tf_op jit(solution)/shard_map/ppermute | solution.py:148
  16.0 10.9 %shard_map.93 = (f32[384,128]{1,0:T(8,128)S(1)}, f32[384,128]{1,0:T(8,128)S(1)}) custom-call(s32[1,2]{1,0:T(1,128)S(4)} %get-tuple-element.16.tiles, s32[96]{0:T(128)S(4)} %get-tuple-element.17.place, f32[192,128]{1,0:T(8,128)S(1)} %constant_dynamic-update-slice_fusion.after.refs_0_, f32[192,128]{1,0:T(8,128)S(1)} %collective-permute-done.3.refs_1_, ...), custom_call_target="tpu_custom_call" | custom-call | flops 7247757312 | bytes 9437184 | tf_op jit(solution)/shard_map/pallas_call | solution.py:387
  26.8 0.2 collective-permute-start.6
  27.1 1.3 %collective-permute-done.6 = f32[384,128]{1,0:T(8,128)S(1)} collective-permute-done((f32[384,128]{1,0:T(8,128)S(1)}, f32[384,128]{1,0:T(8,128)S(1)}, u32[]{:S(2)}, u32[]{:S(2)}) %collective-permute-start.6) | collective-permute-done | bytes 196640 | tf_op jit(solution)/shard_map/ppermute | solution.py:156
  28.4 0.1 collective-permute-start.7
  28.5 3.5 %collective-permute-start.9 = (f32[96,128]{1,0:T(8,128)S(1)}, f32[96,128]{1,0:T(8,128)S(1)}, u32[]{:S(2)}, u32[]{:S(2)}) collective-permute-start(f32[96,128]{1,0:T(8,128)S(1)} %get-tuple-element.28), channel_id=1, source_target_pairs={{0,12},{4,8},{8,4},{12,0},{1,13},{5,9},{9,5},{13,1},{2,14},{6,10},... | collective-permute-start | bytes 147464 | tf_op jit(solution)/shard_map/ppermute | solution.py:160
  32.0 0.0 collective-permute-start.8
  32.0 0.6 %collective-permute-done.7 = f32[96,128]{1,0:T(8,128)S(1)} collective-permute-done((f32[96,128]{1,0:T(8,128)S(1)}, f32[96,128]{1,0:T(8,128)S(1)}, u32[]{:S(2)}, u32[]{:S(2)}) %collective-permute-start.7) | collective-permute-done | bytes 49184 | tf_op jit(solution)/shard_map/ppermute | solution.py:160
  32.6 2.8 %collective-permute-done.9 = f32[96,128]{1,0:T(8,128)S(1)} collective-permute-done((f32[96,128]{1,0:T(8,128)S(1)}, f32[96,128]{1,0:T(8,128)S(1)}, u32[]{:S(2)}, u32[]{:S(2)}) %collective-permute-start.9) | collective-permute-done | bytes 49184 | tf_op jit(solution)/shard_map/ppermute | solution.py:160
  35.3 1.6 %collective-permute-done.8 = f32[96,128]{1,0:T(8,128)S(1)} collective-permute-done((f32[96,128]{1,0:T(8,128)S(1)}, f32[96,128]{1,0:T(8,128)S(1)}, u32[]{:S(2)}, u32[]{:S(2)}) %collective-permute-start.8) | collective-permute-done | bytes 49184 | tf_op jit(solution)/shard_map/ppermute | solution.py:160
  37.0 1.6 %collective-permute-start.10 = (f32[48,128]{1,0:T(8,128)S(1)}, f32[48,128]{1,0:T(8,128)S(1)}, u32[]{:S(2)}, u32[]{:S(2)}) collective-permute-start(f32[48,128]{1,0:T(8,128)S(1)} %slice.29), channel_id=1, source_target_pairs={{0,2},{1,3},{2,0},{3,1},{4,6},{5,7},{6,4},{7,5},{8,10},{9,11},{10,... | collective-permute-start | bytes 73736 | tf_op jit(solution)/shard_map/ppermute | solution.py:168
  38.6 2.3 %collective-permute-done.10 = f32[48,128]{1,0:T(8,128)S(1)} collective-permute-done((f32[48,128]{1,0:T(8,128)S(1)}, f32[48,128]{1,0:T(8,128)S(1)}, u32[]{:S(2)}, u32[]{:S(2)}) %collective-permute-start.10) | collective-permute-done | bytes 24608 | tf_op jit(solution)/shard_map/ppermute | solution.py:168
  40.9 0.6 %slice_add_fusion.1 = f32[48,128]{1,0:T(8,128)} fusion(f32[48,128]{1,0:T(8,128)S(1)} %collective-permute-done.10, f32[96,128]{1,0:T(8,128)S(1)} %fusion.1), kind=kLoop, calls=%fused_computation.3 | loop fusion | flops 6144 | bytes 73728 | tf_op jit(solution)/shard_map/add | solution.py:168
  (8 shorter events, 0.1 us)
Async XLA Ops:
  0.0 10.0 %collective-permute-start.2 = (f32[48,128]{1,0:T(8,128)}, f32[48,128]{1,0:T(8,128)S(1)}, u32[]{:S(2)}, u32[]{:S(2)}) collective-permute-start(f32[48,128]{1,0:T(8,128)} %bitcast.4), channel_id=1, source_target_pairs={{0,12},{4,8},{8,4},{12,0},{1,13},{5,9},{9,5},{13,1},{2,14},{6,10},... | collective-permute-start | bytes 73736 | tf_op jit(solution)/shard_map/ppermute | solution.py:145
  5.0 4.9 %collective-permute-start.1 = (f32[48,128]{1,0:T(8,128)}, f32[48,128]{1,0:T(8,128)S(1)}, u32[]{:S(2)}, u32[]{:S(2)}) collective-permute-start(f32[48,128]{1,0:T(8,128)} %bitcast.5), channel_id=1, source_target_pairs={{0,8},{4,12},{8,0},{12,4},{1,9},{5,13},{9,1},{13,5},{2,10},{6,14},... | collective-permute-start | bytes 73736 | tf_op jit(solution)/shard_map/ppermute | solution.py:145
  5.1 4.0 %collective-permute-start = (f32[48,128]{1,0:T(8,128)}, f32[48,128]{1,0:T(8,128)S(1)}, u32[]{:S(2)}, u32[]{:S(2)}) collective-permute-start(f32[48,128]{1,0:T(8,128)} %bitcast.6), channel_id=1, source_target_pairs={{0,4},{4,0},{8,12},{12,8},{1,5},{5,1},{9,13},{13,9},{2,6},{6,2},{1... | collective-permute-start | bytes 73736 | tf_op jit(solution)/shard_map/ppermute | solution.py:145
  10.0 4.7 %collective-permute-start.3 = (f32[192,128]{1,0:T(8,128)S(1)}, f32[192,128]{1,0:T(8,128)S(1)}, u32[]{:S(2)}, u32[]{:S(2)}) collective-permute-start(f32[192,128]{1,0:T(8,128)S(1)} %constant_dynamic-update-slice_fusion.after.refs_0_), channel_id=1, source_target_pairs={{0,2},{1,3},{2,0},{3,1},{4,6},{5,7},{6,4},{7,5},{8,10},{9,11},{10,... | collective-permute-start | bytes 294920 | tf_op jit(solution)/shard_map/ppermute | solution.py:148
  11.6 3.9 %collective-permute-start.4 = (f32[192,128]{1,0:T(8,128)S(1)}, f32[192,128]{1,0:T(8,128)S(1)}, u32[]{:S(2)}, u32[]{:S(2)}) collective-permute-start(f32[192,128]{1,0:T(8,128)S(1)} %constant_dynamic-update-slice_fusion.after.refs_0_), channel_id=1, source_target_pairs={{0,1},{1,0},{2,3},{3,2},{4,5},{5,4},{6,7},{7,6},{8,9},{9,8},{10,11... | collective-permute-start | bytes 294920 | tf_op jit(solution)/shard_map/ppermute | solution.py:148
  14.7 1.3 %collective-permute-start.5 = (f32[192,128]{1,0:T(8,128)S(1)}, f32[192,128]{1,0:T(8,128)S(1)}, u32[]{:S(2)}, u32[]{:S(2)}) collective-permute-start(f32[192,128]{1,0:T(8,128)S(1)} %collective-permute-done.3.refs_1_), channel_id=1, source_target_pairs={{0,1},{1,0},{2,3},{3,2},{4,5},{5,4},{6,7},{7,6},{8,9},{9,8},{10,11... | collective-permute-start | bytes 294920 | tf_op jit(solution)/shard_map/ppermute | solution.py:148
  26.8 1.5 %collective-permute-start.6 = (f32[384,128]{1,0:T(8,128)S(1)}, f32[384,128]{1,0:T(8,128)S(1)}, u32[]{:S(2)}, u32[]{:S(2)}) collective-permute-start(f32[384,128]{1,0:T(8,128)S(1)} %get-tuple-element.26), channel_id=1, source_target_pairs={{0,1},{1,0},{2,3},{3,2},{4,5},{5,4},{6,7},{7,6},{8,9},{9,8},{10,11... | collective-permute-start | bytes 589832 | tf_op jit(solution)/shard_map/ppermute | solution.py:156
  28.4 4.2 %collective-permute-start.7 = (f32[96,128]{1,0:T(8,128)S(1)}, f32[96,128]{1,0:T(8,128)S(1)}, u32[]{:S(2)}, u32[]{:S(2)}) collective-permute-start(f32[96,128]{1,0:T(8,128)S(1)} %get-tuple-element.27), channel_id=1, source_target_pairs={{0,4},{4,0},{8,12},{12,8},{1,5},{5,1},{9,13},{13,9},{2,6},{6,2},{1... | collective-permute-start | bytes 147464 | tf_op jit(solution)/shard_map/ppermute | solution.py:160
  28.5 6.8 %collective-permute-start.9 = (f32[96,128]{1,0:T(8,128)S(1)}, f32[96,128]{1,0:T(8,128)S(1)}, u32[]{:S(2)}, u32[]{:S(2)}) collective-permute-start(f32[96,128]{1,0:T(8,128)S(1)} %get-tuple-element.28), channel_id=1, source_target_pairs={{0,12},{4,8},{8,4},{12,0},{1,13},{5,9},{9,5},{13,1},{2,14},{6,10},... | collective-permute-start | bytes 147464 | tf_op jit(solution)/shard_map/ppermute | solution.py:160
  32.0 5.0 %collective-permute-start.8 = (f32[96,128]{1,0:T(8,128)S(1)}, f32[96,128]{1,0:T(8,128)S(1)}, u32[]{:S(2)}, u32[]{:S(2)}) collective-permute-start(f32[96,128]{1,0:T(8,128)S(1)} %get-tuple-element.29), channel_id=1, source_target_pairs={{0,8},{4,12},{8,0},{12,4},{1,9},{5,13},{9,1},{13,5},{2,10},{6,14},... | collective-permute-start | bytes 147464 | tf_op jit(solution)/shard_map/ppermute | solution.py:160
  37.0 3.9 %collective-permute-start.10 = (f32[48,128]{1,0:T(8,128)S(1)}, f32[48,128]{1,0:T(8,128)S(1)}, u32[]{:S(2)}, u32[]{:S(2)}) collective-permute-start(f32[48,128]{1,0:T(8,128)S(1)} %slice.29), channel_id=1, source_target_pairs={{0,2},{1,3},{2,0},{3,1},{4,6},{5,7},{6,4},{7,5},{8,10},{9,11},{10,... | collective-permute-start | bytes 73736 | tf_op jit(solution)/shard_map/ppermute | solution.py:168

commit v6 on v5

--- a/solution.py
+++ b/solution.py
@@ -158,7 +158,7 @@
         each = total.shape[0] // sta
         sent = [
             lax.ppermute(total[k * each : (k + 1) * each], "sta", pairs(sta, k))
-            for k in range(sta - 1, 0, -1)
+            for k in range(1, sta)
         ]
         total = total[:each]
         for part in reversed(sent):

time: 41.7 us -> 40.9 us (0.981)
  waiting for transfers between devices: 14.3 us -> 12.6 us
  starting transfers between devices: 12.5 us -> 13.4 us
    ppermute x3, waiting for transfers between devices: 4.98 us -> 3.32 us  [scatter_sum(): lax.ppermute(total[k * each:(k + 1) * each], 'sta', pairs(sta, k))]
    ppermute x3, starting transfers between devices: 3.58 us -> 4.45 us  [scatter_sum(): lax.ppermute(total[k * each:(k + 1) * each], 'sta', pairs(sta, k))]
  transfers between devices with their start and end apart: 11 -> 11, of which waited for: 9 -> 9; matrix products, arithmetic and copies ran while one was open for 0% -> 0% of each run, Pallas kernels for 7% -> 8%
where the time goes in v6:
time: 40.9 us; the launch traced here: 40.7 us
  Pallas kernels  13.9 us (34%)
  starting transfers between devices  13.4 us (33%)
  waiting for transfers between devices  12.6 us (31%)
  other arithmetic  0.65 us (2%)
    pallas_call x1, Pallas kernels, tile_call(): pl.pallas_call(functools.partial(tile_kernel, geometry, len(held), n_out,...  10.9 us
    ppermute x3, starting transfers between devices, gather(): lax.ppermute(piece, 'sta', pairs(sta, k))  5.62 us
    ppermute x3, starting transfers between devices, scatter_sum(): lax.ppermute(total[k * each:(k + 1) * each], 'sta', pairs(sta, k))  4.45 us
    ppermute x3, waiting for transfers between devices, gather(): held = held + [lax.ppermute(one, 'band', pairs(band, bit)) for one in held]  3.65 us
    ppermute x3, waiting for transfers between devices, scatter_sum(): lax.ppermute(total[k * each:(k + 1) * each], 'sta', pairs(sta, k))  3.32 us
    ppermute x1, waiting for transfers between devices, scatter_sum(): total = total[:half] + lax.ppermute(total[half:], 'band', pairs(band, bit))  2.34 us
    pallas_call x1, Pallas kernels, stage(): pl.pallas_call(stage_kernel, in_specs=[pl.BlockSpec(memory_space=pl.ANY)]...  2.31 us
    ppermute x3, waiting for transfers between devices, gather(): lax.ppermute(piece, 'sta', pairs(sta, k))  2.04 us
  transfers between devices with their start and end apart: 11, of which 9 were waited for; matrix products, arithmetic and copies ran while one was open for 0% of the time, Pallas kernels for 8%

profile of v6, /device:TPU:0, one launch (start us, length us, event | category | flops | bytes accessed | tf_op | source)
XLA Modules:
  0.0 40.7 jit_solution(14337519489475981022)
XLA Ops:
  0.0 5.0 %collective-permute-start.2 = (f32[48,128]{1,0:T(8,128)}, f32[48,128]{1,0:T(8,128)S(1)}, u32[]{:S(2)}, u32[]{:S(2)}) collective-permute-start(f32[48,128]{1,0:T(8,128)} %bitcast.4), channel_id=1, source_target_pairs={{0,12},{4,8},{8,4},{12,0},{1,13},{5,9},{9,5},{13,1},{2,14},{6,10},... | collective-permute-start | bytes 73736 | tf_op jit(solution)/shard_map/ppermute | solution.py:145
  5.0 0.0 collective-permute-start.1
  5.1 0.6 %collective-permute-start = (f32[48,128]{1,0:T(8,128)}, f32[48,128]{1,0:T(8,128)S(1)}, u32[]{:S(2)}, u32[]{:S(2)}) collective-permute-start(f32[48,128]{1,0:T(8,128)} %bitcast.6), channel_id=1, source_target_pairs={{0,4},{4,0},{8,12},{12,8},{1,5},{5,1},{9,13},{13,9},{2,6},{6,2},{1... | collective-permute-start | bytes 73736 | tf_op jit(solution)/shard_map/ppermute | solution.py:145
  5.6 2.3 %shard_map.91 = (f32[48,128]{1,0:T(8,128)S(1)}, f32[48,48,256]{2,1,0:T(8,128)S(1)}, bf16[1024,256]{1,0:T(8,128)(2,1)S(1)}, bf16[1024,256]{1,0:T(8,128)(2,1)S(1)}...) custom-call(f32[48,128]{1,0:T(8,128)} %bitcast.7, ...), custom_call_target="tpu_custom_call" | custom-call | bytes 8896512 | tf_op jit(solution)/shard_map/pallas_call | solution.py:77
  7.9 1.1 %collective-permute-done = f32[48,128]{1,0:T(8,128)S(1)} collective-permute-done((f32[48,128]{1,0:T(8,128)}, f32[48,128]{1,0:T(8,128)S(1)}, u32[]{:S(2)}, u32[]{:S(2)}) %collective-permute-start) | collective-permute-done | bytes 24608 | tf_op jit(solution)/shard_map/ppermute | solution.py:145
  9.1 0.9 %collective-permute-done.1 = f32[48,128]{1,0:T(8,128)S(1)} collective-permute-done((f32[48,128]{1,0:T(8,128)}, f32[48,128]{1,0:T(8,128)S(1)}, u32[]{:S(2)}, u32[]{:S(2)}) %collective-permute-start.1) | collective-permute-done | bytes 24608 | tf_op jit(solution)/shard_map/ppermute | solution.py:145
  10.0 0.0 collective-permute-done.2
  10.0 1.6 %collective-permute-start.3 = (f32[192,128]{1,0:T(8,128)S(1)}, f32[192,128]{1,0:T(8,128)S(1)}, u32[]{:S(2)}, u32[]{:S(2)}) collective-permute-start(f32[192,128]{1,0:T(8,128)S(1)} %constant_dynamic-update-slice_fusion.after.refs_0_), channel_id=1, source_target_pairs={{0,2},{1,3},{2,0},{3,1},{4,6},{5,7},{6,4},{7,5},{8,10},{9,11},{10,... | collective-permute-start | bytes 294920 | tf_op jit(solution)/shard_map/ppermute | solution.py:148
  11.6 0.0 collective-permute-start.4
  11.6 3.1 %collective-permute-done.3.refs_1_ = f32[192,128]{1,0:T(8,128)S(1)} collective-permute-done((f32[192,128]{1,0:T(8,128)S(1)}, f32[192,128]{1,0:T(8,128)S(1)}, u32[]{:S(2)}, u32[]{:S(2)}) %collective-permute-start.3) | collective-permute-done | bytes 98336 | tf_op jit(solution)/shard_map/ppermute | solution.py:148
  14.7 0.0 collective-permute-start.5
  14.7 0.8 %shard_map.92.refs_8_ = f32[48,48,256]{2,1,0:T(8,128)S(1)} custom-call(f32[48,48,256]{2,1,0:T(8,128)S(1)} %get-tuple-element.23.seen, bf16[384,128]{1,0:T(8,128)(2,1)S(1)} %get-tuple-element.24.move, f32[192,128]{1,0:T(8,128)S(1)} %constant_dynamic-update-slice_fusion.after.refs_0_), custom_call_target="tpu_custom_call" | custom-call | flops 452984832 | bytes 4718592 | tf_op jit(solution)/shard_map/pallas_call | solution.py:106
  15.5 0.0 collective-permute-done.4.refs_2_
  15.5 0.5 %collective-permute-done.5.refs_3_ = f32[192,128]{1,0:T(8,128)S(1)} collective-permute-done((f32[192,128]{1,0:T(8,128)S(1)}, f32[192,128]{1,0:T(8,128)S(1)}, u32[]{:S(2)}, u32[]{:S(2)}) %collective-permute-start.5) | collective-permute-done | bytes 98336 | tf_op jit(solution)/shard_map/ppermute | solution.py:148
  16.0 10.9 %shard_map.93 = (f32[384,128]{1,0:T(8,128)S(1)}, f32[384,128]{1,0:T(8,128)S(1)}) custom-call(s32[1,2]{1,0:T(1,128)S(4)} %get-tuple-element.16.tiles, s32[96]{0:T(128)S(4)} %get-tuple-element.17.place, f32[192,128]{1,0:T(8,128)S(1)} %constant_dynamic-update-slice_fusion.after.refs_0_, f32[192,128]{1,0:T(8,128)S(1)} %collective-permute-done.3.refs_1_, ...), custom_call_target="tpu_custom_call" | custom-call | flops 7247757312 | bytes 9437184 | tf_op jit(solution)/shard_map/pallas_call | solution.py:387
  26.9 0.2 collective-permute-start.6
  27.1 1.3 %collective-permute-done.6 = f32[384,128]{1,0:T(8,128)S(1)} collective-permute-done((f32[384,128]{1,0:T(8,128)S(1)}, f32[384,128]{1,0:T(8,128)S(1)}, u32[]{:S(2)}, u32[]{:S(2)}) %collective-permute-start.6) | collective-permute-done | bytes 196640 | tf_op jit(solution)/shard_map/ppermute | solution.py:156
  28.4 1.9 %collective-permute-start.7 = (f32[96,128]{1,0:T(8,128)S(1)}, f32[96,128]{1,0:T(8,128)S(1)}, u32[]{:S(2)}, u32[]{:S(2)}) collective-permute-start(f32[96,128]{1,0:T(8,128)S(1)} %get-tuple-element.27), channel_id=1, source_target_pairs={{0,12},{4,8},{8,4},{12,0},{1,13},{5,9},{9,5},{13,1},{2,14},{6,10},... | collective-permute-start | bytes 147464 | tf_op jit(solution)/shard_map/ppermute | solution.py:160
  30.3 0.8 %collective-permute-start.9 = (f32[96,128]{1,0:T(8,128)S(1)}, f32[96,128]{1,0:T(8,128)S(1)}, u32[]{:S(2)}, u32[]{:S(2)}) collective-permute-start(f32[96,128]{1,0:T(8,128)S(1)} %get-tuple-element.28), channel_id=1, source_target_pairs={{0,4},{4,0},{8,12},{12,8},{1,5},{5,1},{9,13},{13,9},{2,6},{6,2},{1... | collective-permute-start | bytes 147464 | tf_op jit(solution)/shard_map/ppermute | solution.py:160
  31.1 1.8 %collective-permute-start.8 = (f32[96,128]{1,0:T(8,128)S(1)}, f32[96,128]{1,0:T(8,128)S(1)}, u32[]{:S(2)}, u32[]{:S(2)}) collective-permute-start(f32[96,128]{1,0:T(8,128)S(1)} %get-tuple-element.29), channel_id=1, source_target_pairs={{0,8},{4,12},{8,0},{12,4},{1,9},{5,13},{9,1},{13,5},{2,10},{6,14},... | collective-permute-start | bytes 147464 | tf_op jit(solution)/shard_map/ppermute | solution.py:160
  32.9 1.9 %collective-permute-done.7 = f32[96,128]{1,0:T(8,128)S(1)} collective-permute-done((f32[96,128]{1,0:T(8,128)S(1)}, f32[96,128]{1,0:T(8,128)S(1)}, u32[]{:S(2)}, u32[]{:S(2)}) %collective-permute-start.7) | collective-permute-done | bytes 49184 | tf_op jit(solution)/shard_map/ppermute | solution.py:160
  34.8 0.7 %collective-permute-done.9 = f32[96,128]{1,0:T(8,128)S(1)} collective-permute-done((f32[96,128]{1,0:T(8,128)S(1)}, f32[96,128]{1,0:T(8,128)S(1)}, u32[]{:S(2)}, u32[]{:S(2)}) %collective-permute-start.9) | collective-permute-done | bytes 49184 | tf_op jit(solution)/shard_map/ppermute | solution.py:160
  35.4 0.8 %collective-permute-done.8 = f32[96,128]{1,0:T(8,128)S(1)} collective-permute-done((f32[96,128]{1,0:T(8,128)S(1)}, f32[96,128]{1,0:T(8,128)S(1)}, u32[]{:S(2)}, u32[]{:S(2)}) %collective-permute-start.8) | collective-permute-done | bytes 49184 | tf_op jit(solution)/shard_map/ppermute | solution.py:160
  36.2 1.6 %collective-permute-start.10 = (f32[48,128]{1,0:T(8,128)S(1)}, f32[48,128]{1,0:T(8,128)S(1)}, u32[]{:S(2)}, u32[]{:S(2)}) collective-permute-start(f32[48,128]{1,0:T(8,128)S(1)} %slice.29), channel_id=1, source_target_pairs={{0,2},{1,3},{2,0},{3,1},{4,6},{5,7},{6,4},{7,5},{8,10},{9,11},{10,... | collective-permute-start | bytes 73736 | tf_op jit(solution)/shard_map/ppermute | solution.py:168
  37.8 2.3 %collective-permute-done.10 = f32[48,128]{1,0:T(8,128)S(1)} collective-permute-done((f32[48,128]{1,0:T(8,128)S(1)}, f32[48,128]{1,0:T(8,128)S(1)}, u32[]{:S(2)}, u32[]{:S(2)}) %collective-permute-start.10) | collective-permute-done | bytes 24608 | tf_op jit(solution)/shard_map/ppermute | solution.py:168
  40.1 0.6 %slice_add_fusion.1 = f32[48,128]{1,0:T(8,128)} fusion(f32[48,128]{1,0:T(8,128)S(1)} %collective-permute-done.10, f32[96,128]{1,0:T(8,128)S(1)} %fusion.1), kind=kLoop, calls=%fused_computation.3 | loop fusion | flops 6144 | bytes 73728 | tf_op jit(solution)/shard_map/add | solution.py:168
  (8 shorter events, 0.1 us)
Async XLA Ops:
  0.0 10.0 %collective-permute-start.2 = (f32[48,128]{1,0:T(8,128)}, f32[48,128]{1,0:T(8,128)S(1)}, u32[]{:S(2)}, u32[]{:S(2)}) collective-permute-start(f32[48,128]{1,0:T(8,128)} %bitcast.4), channel_id=1, source_target_pairs={{0,12},{4,8},{8,4},{12,0},{1,13},{5,9},{9,5},{13,1},{2,14},{6,10},... | collective-permute-start | bytes 73736 | tf_op jit(solution)/shard_map/ppermute | solution.py:145
  5.0 4.9 %collective-permute-start.1 = (f32[48,128]{1,0:T(8,128)}, f32[48,128]{1,0:T(8,128)S(1)}, u32[]{:S(2)}, u32[]{:S(2)}) collective-permute-start(f32[48,128]{1,0:T(8,128)} %bitcast.5), channel_id=1, source_target_pairs={{0,8},{4,12},{8,0},{12,4},{1,9},{5,13},{9,1},{13,5},{2,10},{6,14},... | collective-permute-start | bytes 73736 | tf_op jit(solution)/shard_map/ppermute | solution.py:145
  5.1 4.0 %collective-permute-start = (f32[48,128]{1,0:T(8,128)}, f32[48,128]{1,0:T(8,128)S(1)}, u32[]{:S(2)}, u32[]{:S(2)}) collective-permute-start(f32[48,128]{1,0:T(8,128)} %bitcast.6), channel_id=1, source_target_pairs={{0,4},{4,0},{8,12},{12,8},{1,5},{5,1},{9,13},{13,9},{2,6},{6,2},{1... | collective-permute-start | bytes 73736 | tf_op jit(solution)/shard_map/ppermute | solution.py:145
  10.0 4.7 %collective-permute-start.3 = (f32[192,128]{1,0:T(8,128)S(1)}, f32[192,128]{1,0:T(8,128)S(1)}, u32[]{:S(2)}, u32[]{:S(2)}) collective-permute-start(f32[192,128]{1,0:T(8,128)S(1)} %constant_dynamic-update-slice_fusion.after.refs_0_), channel_id=1, source_target_pairs={{0,2},{1,3},{2,0},{3,1},{4,6},{5,7},{6,4},{7,5},{8,10},{9,11},{10,... | collective-permute-start | bytes 294920 | tf_op jit(solution)/shard_map/ppermute | solution.py:148
  11.6 3.9 %collective-permute-start.4 = (f32[192,128]{1,0:T(8,128)S(1)}, f32[192,128]{1,0:T(8,128)S(1)}, u32[]{:S(2)}, u32[]{:S(2)}) collective-permute-start(f32[192,128]{1,0:T(8,128)S(1)} %constant_dynamic-update-slice_fusion.after.refs_0_), channel_id=1, source_target_pairs={{0,1},{1,0},{2,3},{3,2},{4,5},{5,4},{6,7},{7,6},{8,9},{9,8},{10,11... | collective-permute-start | bytes 294920 | tf_op jit(solution)/shard_map/ppermute | solution.py:148
  14.7 1.3 %collective-permute-start.5 = (f32[192,128]{1,0:T(8,128)S(1)}, f32[192,128]{1,0:T(8,128)S(1)}, u32[]{:S(2)}, u32[]{:S(2)}) collective-permute-start(f32[192,128]{1,0:T(8,128)S(1)} %collective-permute-done.3.refs_1_), channel_id=1, source_target_pairs={{0,1},{1,0},{2,3},{3,2},{4,5},{5,4},{6,7},{7,6},{8,9},{9,8},{10,11... | collective-permute-start | bytes 294920 | tf_op jit(solution)/shard_map/ppermute | solution.py:148
  26.9 1.5 %collective-permute-start.6 = (f32[384,128]{1,0:T(8,128)S(1)}, f32[384,128]{1,0:T(8,128)S(1)}, u32[]{:S(2)}, u32[]{:S(2)}) collective-permute-start(f32[384,128]{1,0:T(8,128)S(1)} %get-tuple-element.26), channel_id=1, source_target_pairs={{0,1},{1,0},{2,3},{3,2},{4,5},{5,4},{6,7},{7,6},{8,9},{9,8},{10,11... | collective-permute-start | bytes 589832 | tf_op jit(solution)/shard_map/ppermute | solution.py:156
  28.4 6.3 %collective-permute-start.7 = (f32[96,128]{1,0:T(8,128)S(1)}, f32[96,128]{1,0:T(8,128)S(1)}, u32[]{:S(2)}, u32[]{:S(2)}) collective-permute-start(f32[96,128]{1,0:T(8,128)S(1)} %get-tuple-element.27), channel_id=1, source_target_pairs={{0,12},{4,8},{8,4},{12,0},{1,13},{5,9},{9,5},{13,1},{2,14},{6,10},... | collective-permute-start | bytes 147464 | tf_op jit(solution)/shard_map/ppermute | solution.py:160
  30.3 5.1 %collective-permute-start.9 = (f32[96,128]{1,0:T(8,128)S(1)}, f32[96,128]{1,0:T(8,128)S(1)}, u32[]{:S(2)}, u32[]{:S(2)}) collective-permute-start(f32[96,128]{1,0:T(8,128)S(1)} %get-tuple-element.28), channel_id=1, source_target_pairs={{0,4},{4,0},{8,12},{12,8},{1,5},{5,1},{9,13},{13,9},{2,6},{6,2},{1... | collective-permute-start | bytes 147464 | tf_op jit(solution)/shard_map/ppermute | solution.py:160
  31.1 5.1 %collective-permute-start.8 = (f32[96,128]{1,0:T(8,128)S(1)}, f32[96,128]{1,0:T(8,128)S(1)}, u32[]{:S(2)}, u32[]{:S(2)}) collective-permute-start(f32[96,128]{1,0:T(8,128)S(1)} %get-tuple-element.29), channel_id=1, source_target_pairs={{0,8},{4,12},{8,0},{12,4},{1,9},{5,13},{9,1},{13,5},{2,10},{6,14},... | collective-permute-start | bytes 147464 | tf_op jit(solution)/shard_map/ppermute | solution.py:160
  36.2 3.9 %collective-permute-start.10 = (f32[48,128]{1,0:T(8,128)S(1)}, f32[48,128]{1,0:T(8,128)S(1)}, u32[]{:S(2)}, u32[]{:S(2)}) collective-permute-start(f32[48,128]{1,0:T(8,128)S(1)} %slice.29), channel_id=1, source_target_pairs={{0,2},{1,3},{2,0},{3,1},{4,6},{5,7},{6,4},{7,5},{8,10},{9,11},{10,... | collective-permute-start | bytes 73736 | tf_op jit(solution)/shard_map/ppermute | solution.py:168
